TPU v7x, 256 devices: a whole 4x4x8 slice. The times are simulated.
256 devices in a mesh: dp: 128 (over x, y_hi, z, core), pair: 2 (over y_lo).
Axes of the slice: x: 4, y: 4 (y_hi: 2, y_lo: 2; y = y_hi * 2 + y_lo), z: 8, core: 2. Of those that a mesh axis runs over, the one named last changes fastest.
Arguments:
- tokens: bfloat16 [24576, 1792], P('dp'), may hold values from -6 to 6
- grad_out: bfloat16 [24576, 1792], P('dp'), may hold values from -6 to 6
- gate_probs: bfloat16 [24576, 2], P('dp'), may hold values from 0.049804688 to 1
- expert_ids: int32 [24576, 2], P('dp'), may hold values from 0 to 64, as said below
- route_slots: int32 [24576, 2], P('dp'), may hold values from 0 to 191, as said below
- hot_flags: int32 [65], replicated, may hold values from 0 to 1, as said below
- owner_slot: int32 [65], replicated, may hold values from 0 to 63, as said below
- cold_gate: bfloat16 [128, 640, 1792], P('dp', 'pair'), may hold values from -0.125 to 0.125
- cold_up: bfloat16 [128, 640, 1792], P('dp', 'pair'), may hold values from -0.125 to 0.125
- cold_down: bfloat16 [128, 640, 1792], P('dp', 'pair'), may hold values from -0.15625 to 0.15625
- hot_gate: bfloat16 [1280, 1792], P(('dp', 'pair')), may hold values from -0.125 to 0.125
- hot_up: bfloat16 [1280, 1792], P(('dp', 'pair')), may hold values from -0.125 to 0.125
- hot_down: bfloat16 [1280, 1792], P(('dp', 'pair')), may hold values from -0.15625 to 0.15625
Outputs:
- grad_tokens: bfloat16 [24576, 1792], P(('dp', 'pair'))
- grad_probs: float32 [24576, 2], P(('dp', 'pair'))
- grad_cold_gate: bfloat16 [128, 640, 1792], P('dp', 'pair')
- grad_cold_up: bfloat16 [128, 640, 1792], P('dp', 'pair')
- grad_cold_down: bfloat16 [128, 640, 1792], P('dp', 'pair')
- grad_hot_gate: bfloat16 [1280, 1792], P(('dp', 'pair'))
- grad_hot_up: bfloat16 [1280, 1792], P(('dp', 'pair'))
- grad_hot_down: bfloat16 [1280, 1792], P(('dp', 'pair'))
Inputs may be any that keep to these rules, and one draw needn't show every extreme that they name: `expert_ids`: each token names 2 different experts; on every device at least 48 tokens name the hot expert, on some device all of them do, and some cold expert is named by 4 or more tokens. `route_slots`: on one device the routes to one expert carry the slots 0, 1, 2 and so on, each once. `hot_flags`: exactly one entry is 1. `owner_slot`: the cold experts hold the slots 0 to 63, each once; the hot expert's entry is 0.
All inputs are finite; a program needn't handle non-finite values.
Results may differ from a plain program's by a relative error of at most 0.0049.
Values may be sent and summed in bfloat16 or wider, within the bound.
A program may use at most 192 MiB of HBM per device.

v0:
```python
import jax
import jax.numpy as jnp
from jax import lax
from jax.sharding import PartitionSpec as P

TOP = 2
CAP = 4
HCAP = 48


contract_rows = (((0,), (0,)), ((), ()))


def expert_back(rows_in, rows_grad, rows_gate, w_gate, w_up, w_down):
    pre_gate = jnp.dot(rows_in, w_gate.T, preferred_element_type=jnp.float32)
    pre_up = jnp.dot(rows_in, w_up.T, preferred_element_type=jnp.float32)
    back_proj = jnp.dot(rows_grad, w_down.T, preferred_element_type=jnp.float32)
    sigmoid_gate = 1.0 / (1.0 + jnp.exp(-pre_gate))
    activation = pre_gate * sigmoid_gate
    hidden = activation * pre_up
    prob_grad = jnp.sum(hidden * back_proj, axis=1)
    gate_scale = rows_gate.astype(jnp.float32)[:, None]
    hidden_grad = gate_scale * back_proj
    gate_grad = (
        hidden_grad * pre_up * sigmoid_gate * (1.0 + pre_gate * (1.0 - sigmoid_gate))
    ).astype(jnp.bfloat16)
    up_grad = (hidden_grad * activation).astype(jnp.bfloat16)
    weighted = (gate_scale * hidden).astype(jnp.bfloat16)
    input_grad = jnp.dot(gate_grad, w_gate, preferred_element_type=jnp.float32) + jnp.dot(
        up_grad, w_up, preferred_element_type=jnp.float32
    )
    return (gate_grad, up_grad, weighted, input_grad, prob_grad)


def lookup(flat_ids, table_values, entries):
    onehot = flat_ids[:, None] == jnp.arange(entries, dtype=jnp.int32)[None, :]
    return jnp.sum(jnp.where(onehot, table_values[None, :], 0), axis=1)


def pick_rows(route_table, tokens, grad_out, flat_gate):
    token_index = route_table // TOP
    rows_in = jnp.take(tokens, token_index, axis=0, mode="fill", fill_value=0)
    rows_grad = jnp.take(grad_out, token_index, axis=0, mode="fill", fill_value=0)
    rows_gate = jnp.take(flat_gate, route_table, axis=0, mode="fill", fill_value=0)
    return (token_index, rows_in, rows_grad, rows_gate)


def local(
    tokens,
    grad_out,
    gate_probs,
    expert_ids,
    route_slots,
    hot_flags,
    owner_slot,
    cold_gate,
    cold_up,
    cold_down,
    hot_gate,
    hot_up,
    hot_down,
):
    device_count = lax.axis_size("dp")
    slot_count = device_count // 2
    token_count = tokens.shape[0]
    model_width = tokens.shape[1]
    route_count = token_count * TOP
    expert_count = hot_flags.shape[0]
    flat_ids = expert_ids.reshape(-1)
    flat_slots = route_slots.reshape(-1)
    flat_gate = gate_probs.reshape(-1)
    routes = jnp.arange(route_count, dtype=jnp.int32)
    is_hot = lookup(flat_ids, hot_flags, expert_count)
    owners = lookup(flat_ids, owner_slot, expert_count)
    live_cold = (is_hot == 0) & (flat_slots < CAP)
    live_hot = (is_hot == 1) & (flat_slots < HCAP)
    cold_pos = jnp.where(live_cold, owners * CAP + flat_slots, slot_count * CAP)
    cold_table = (
        jnp.full((slot_count * CAP,), route_count, jnp.int32).at[cold_pos].set(routes, mode="drop")
    )
    hot_pos = jnp.where(live_hot, flat_slots, HCAP)
    hot_table = jnp.full((HCAP,), route_count, jnp.int32).at[hot_pos].set(routes, mode="drop")
    hot_weights = (
        lax.all_gather(hot_gate, "dp", axis=0, tiled=True),
        lax.all_gather(hot_up, "dp", axis=0, tiled=True),
        lax.all_gather(hot_down, "dp", axis=0, tiled=True),
    )
    cold_tokens, cold_in, cold_grad, cold_prob = pick_rows(cold_table, tokens, grad_out, flat_gate)

    def doubled(rows):
        shaped = rows.reshape((slot_count, 1, CAP) + rows.shape[1:])
        spread = jnp.broadcast_to(shaped, (slot_count, 2, CAP) + rows.shape[1:])
        return spread.reshape((device_count, CAP) + rows.shape[1:])

    send_in = doubled(cold_in)
    send_grad = doubled(cold_grad)
    send_gate = doubled(cold_prob)
    got_in, got_grad, got_gate = (
        lax.all_to_all(send_in, "dp", split_axis=0, concat_axis=0, tiled=True),
        lax.all_to_all(send_grad, "dp", split_axis=0, concat_axis=0, tiled=True),
        lax.all_to_all(send_gate, "dp", split_axis=0, concat_axis=0, tiled=True),
    )
    row_total = device_count * CAP
    owner_in = got_in.reshape(row_total, model_width)
    owner_grad = got_grad.reshape(row_total, model_width)
    owner_gate = got_gate.reshape(row_total)
    gate_grad, up_grad, weighted, owner_dx, owner_dp = expert_back(
        owner_in, owner_grad, owner_gate, cold_gate[0], cold_up[0], cold_down[0]
    )
    grad_cold_gate = lax.dot_general(
        gate_grad, owner_in, contract_rows, preferred_element_type=jnp.float32
    ).astype(jnp.bfloat16)[None]
    grad_cold_up = lax.dot_general(
        up_grad, owner_in, contract_rows, preferred_element_type=jnp.float32
    ).astype(jnp.bfloat16)[None]
    grad_cold_down = lax.dot_general(
        weighted, owner_grad, contract_rows, preferred_element_type=jnp.float32
    ).astype(jnp.bfloat16)[None]
    back_dx, back_dp = (
        lax.all_to_all(
            owner_dx.reshape(device_count, CAP, model_width),
            "dp",
            split_axis=0,
            concat_axis=0,
            tiled=True,
        ),
        lax.all_to_all(
            owner_dp.reshape(device_count, CAP), "dp", split_axis=0, concat_axis=0, tiled=True
        ),
    )
    cold_dx = jnp.sum(back_dx.reshape(slot_count, 2, CAP, model_width), axis=1).reshape(
        slot_count * CAP, model_width
    )
    cold_dp = jnp.sum(back_dp.reshape(slot_count, 2, CAP), axis=1).reshape(slot_count * CAP)
    hot_tokens, hot_in, hot_grad, hot_rows_gate = pick_rows(hot_table, tokens, grad_out, flat_gate)
    full_gate, full_up, full_down = hot_weights
    hot_gate_grad, hot_up_grad, hot_weighted, hot_dx, hot_dp = expert_back(
        hot_in, hot_grad, hot_rows_gate, full_gate, full_up, full_down
    )
    term_gate = lax.dot_general(
        hot_gate_grad, hot_in, contract_rows, preferred_element_type=jnp.float32
    )
    term_up = lax.dot_general(
        hot_up_grad, hot_in, contract_rows, preferred_element_type=jnp.float32
    )
    term_down = lax.dot_general(
        hot_weighted, hot_grad, contract_rows, preferred_element_type=jnp.float32
    )
    hot_sums = lax.psum_scatter(
        jnp.concatenate([term_gate, term_up, term_down], axis=1),
        "dp",
        scatter_dimension=0,
        tiled=True,
    )
    grad_hot_gate = hot_sums[:, :model_width].astype(jnp.bfloat16)
    grad_hot_up = hot_sums[:, model_width : 2 * model_width].astype(jnp.bfloat16)
    grad_hot_down = hot_sums[:, 2 * model_width :].astype(jnp.bfloat16)
    input_total = jnp.zeros((token_count, model_width), jnp.float32)
    input_total = input_total.at[cold_tokens].add(cold_dx, mode="drop")
    input_total = input_total.at[hot_tokens].add(hot_dx, mode="drop")
    route_grad = jnp.zeros((route_count,), jnp.float32)
    route_grad = route_grad.at[cold_table].add(cold_dp, mode="drop")
    route_grad = route_grad.at[hot_table].add(hot_dp, mode="drop")
    summed_dx, summed_dp = (
        lax.psum_scatter(input_total, "pair", scatter_dimension=0, tiled=True),
        lax.psum_scatter(
            route_grad.reshape(token_count, TOP), "pair", scatter_dimension=0, tiled=True
        ),
    )
    return (
        summed_dx.astype(jnp.bfloat16),
        summed_dp,
        grad_cold_gate,
        grad_cold_up,
        grad_cold_down,
        grad_hot_gate,
        grad_hot_up,
        grad_hot_down,
    )


def solution(mesh):
    return jax.shard_map(
        local,
        mesh=mesh,
        in_specs=(
            P("dp", None),
            P("dp", None),
            P("dp", None),
            P("dp", None),
            P("dp", None),
            P(),
            P(),
            P("dp", "pair", None),
            P("dp", "pair", None),
            P("dp", "pair", None),
            P(("dp", "pair"), None),
            P(("dp", "pair"), None),
            P(("dp", "pair"), None),
        ),
        out_specs=(
            P(("dp", "pair"), None),
            P(("dp", "pair"), None),
            P("dp", "pair", None),
            P("dp", "pair", None),
            P("dp", "pair", None),
            P(("dp", "pair"), None),
            P(("dp", "pair"), None),
            P(("dp", "pair"), None),
        ),
        check_vma=False,
    )
```

profile of v0, /device:TPU:1, one launch (start us, length us, event | category | flops | bytes accessed | tf_op | source)
XLA Modules:
  0.0 1169.1 jit_solution(17662097787075045569)
XLA Ops:
  11.7 2.9 scatter_custom_fusion
  17.4 16.4 %all-to-all-start = ((bf16[128,1,4]{2,1,0:T(2,128)(2,1)}), bf16[128,1,4]{2,1,0:T(2,128)(2,1)S(1)}, u32[]{:S(2)}, u32[]{:S(2)}) async-start(bf16[128,1,4]{2,1,0:T(2,128)(2,1)} %copy.39), calls=%async_computation | async-start | bytes 131072 | tf_op jit(solution)/shard_map/all_to_all | solution.py:101
  35.2 2.3 gather_fusion.3
  37.5 2.7 broadcast_select_fusion.1
  41.9 4.0 all-to-all-done
  47.8 10.3 all-to-all-start.2
  60.0 46.1 %all-to-all-done.2 = bf16[128,4,1792]{2,1,0:T(4,128)(2,1)} async-done(((bf16[128,4,1792]{2,1,0:T(4,128)(2,1)}), bf16[128,4,1792]{2,1,0:T(4,128)(2,1)}, u32[]{:S(2)}, u32[]{:S(2)}) %all-to-all-start.2) | async-done | bytes 1835040 | tf_op jit(solution)/shard_map/all_to_all | solution.py:99
  106.2 2.9 broadcast_in_dim.117
  109.0 8.1 all-to-all-start.1
  118.2 4.0 reshape.209
  122.1 3.6 fusion.8
  127.4 38.9 %all-to-all-done.1 = bf16[128,4,1792]{2,1,0:T(4,128)(2,1)} async-done(((bf16[128,4,1792]{2,1,0:T(4,128)(2,1)}), bf16[128,4,1792]{2,1,0:T(4,128)(2,1)}, u32[]{:S(2)}, u32[]{:S(2)}) %all-to-all-start.1) | async-done | bytes 1835040 | tf_op jit(solution)/shard_map/all_to_all | solution.py:100
  166.3 4.0 reshape.207
  170.3 3.2 multiply_reduce_fusion
  174.2 8.6 all-to-all-start.4
  184.1 2.9 convolution_add_fusion
  187.0 5.1 reshape.210
  192.1 2.9 all-to-all-done.4
  195.0 11.3 all-to-all-start.3
  206.4 3.1 scatter_custom_fusion.2
  213.0 3.4 fusion
  220.8 2.3 scatter_custom_fusion.4
  223.1 5.4 reshape.326
  228.5 41.6 %all-gather.11.cloned.1.call-done = bf16[128,5,1792]{2,1,0:T(8,128)(2,1)} async-done(((bf16[1,5,1792]{2,1,0:T(8,128)(2,1)}), bf16[128,5,1792]{2,1,0:T(8,128)(2,1)}) %all-gather.11.cloned.1.call-update) | async-done | bytes 2293776 | tf_op jit(solution)/shard_map/all_gather | solution.py:84
  270.1 5.4 reshape.328
  275.5 115.6 %all-gather.7.cloned.1.call-done = bf16[128,5,1792]{2,1,0:T(8,128)(2,1)} async-done(((bf16[1,5,1792]{2,1,0:T(8,128)(2,1)}), bf16[128,5,1792]{2,1,0:T(8,128)(2,1)}) %all-gather.7.cloned.1.call-update) | async-done | bytes 2293776 | tf_op jit(solution)/shard_map/all_gather | solution.py:86
  391.1 5.4 reshape.324
  396.4 2.6 fusion.37
  406.1 5.3 pad_maximum_fusion
  413.5 3.3 bitcast_reduce_fusion
  418.6 4.7 scatter_custom_fusion.1
  426.2 731.1 %all-reduce.2 = bf16[640,5376]{1,0:T(8,128)(2,1)} all-reduce(f32[640,5376]{1,0:T(8,128)} %pad_maximum_fusion), channel_id=4, replica_groups=mesh['dp'=128,'pair'=2] {'dp'}, use_global_device_ids=true, to_apply=%region_14.17.clone | all-reduce | flops 3440640 | bytes 20643840
  (106 shorter events, 44.5 us)
Async XLA Ops:
  7.2 118.6 %copy-start = (bf16[1,320,1792]{2,1,0:T(8,128)(2,1)S(1)}, bf16[1,320,1792]{2,1,0:T(8,128)(2,1)}, u32[]{:S(2)}) copy-start(bf16[1,320,1792]{2,1,0:T(8,128)(2,1)} %param.24) | copy-start | bytes 3440644
  7.2 26.6 %copy-start.3 = (bf16[192,1792]{1,0:T(8,128)(2,1)S(1)}, bf16[192,1792]{1,0:T(8,128)(2,1)}, u32[]{:S(2)}) copy-start(bf16[192,1792]{1,0:T(8,128)(2,1)} %param.18) | copy-start | bytes 2064388
  7.2 215.9 %all-gather.9.cloned.1.call-start = ((), (), s32[]{:S(2)}) async-start(), calls=%async_computation.10 | async-start | bytes 3698688 | tf_op jit(solution)/shard_map/all_gather | solution.py:85
  17.4 28.6 %all-to-all-start = ((bf16[128,1,4]{2,1,0:T(2,128)(2,1)}), bf16[128,1,4]{2,1,0:T(2,128)(2,1)S(1)}, u32[]{:S(2)}, u32[]{:S(2)}) async-start(bf16[128,1,4]{2,1,0:T(2,128)(2,1)} %copy.39), calls=%async_computation | async-start | bytes 131072 | tf_op jit(solution)/shard_map/all_to_all | solution.py:101
  33.8 1.4 copy-start.2
  47.8 11.1 copy-start.9
  47.8 58.4 %all-to-all-start.2 = ((bf16[128,4,1792]{2,1,0:T(4,128)(2,1)}), bf16[128,4,1792]{2,1,0:T(4,128)(2,1)}, u32[]{:S(2)}, u32[]{:S(2)}) async-start(bf16[128,4,1792]{2,1,0:T(4,128)(2,1)} %bitcast.52), calls=%async_computation.2 | async-start | bytes 3670016 | tf_op jit(solution)/shard_map/all_to_all | solution.py:99
  58.1 212.0 %all-gather.11.cloned.1.call-start = ((), (), s32[]{:S(2)}) async-start(), calls=%async_computation.11 | async-start | bytes 3698688 | tf_op jit(solution)/shard_map/all_gather | solution.py:84
  109.0 57.3 %all-to-all-start.1 = ((bf16[128,4,1792]{2,1,0:T(4,128)(2,1)}), bf16[128,4,1792]{2,1,0:T(4,128)(2,1)}, u32[]{:S(2)}, u32[]{:S(2)}) async-start(bf16[128,4,1792]{2,1,0:T(4,128)(2,1)} %bitcast.51), calls=%async_computation.1 | async-start | bytes 3670016 | tf_op jit(solution)/shard_map/all_to_all | solution.py:100
  117.1 273.9 %all-gather.7.cloned.1.call-start = ((), (), s32[]{:S(2)}) async-start(), calls=%async_computation.9 | async-start | bytes 3698688 | tf_op jit(solution)/shard_map/all_gather | solution.py:86
  122.1 3.6 copy-start.10
  174.2 20.7 %all-to-all-start.4 = ((f32[128,1,4]{2,1,0:T(1,128)}), f32[128,1,4]{2,1,0:T(1,128)S(1)}, u32[]{:S(2)}, u32[]{:S(2)}) async-start(f32[128,1,4]{2,1,0:T(1,128)} %bitcast.10), calls=%async_computation.5 | async-start | bytes 131072 | tf_op jit(solution)/shard_map/all_to_all | solution.py:127
  182.8 1.3 copy-start.13
  195.0 218.6 %all-to-all-start.3 = ((f32[128,4,1792]{2,1,0:T(4,128)}), f32[128,4,1792]{2,1,0:T(4,128)}, u32[]{:S(2)}, u32[]{:S(2)}) async-start(f32[128,4,1792]{2,1,0:T(4,128)} %reshape.210), calls=%async_computation.3 | async-start | bytes 7340032 | tf_op jit(solution)/shard_map/all_to_all | solution.py:120
  206.3 5.5 copy-start.14
  206.3 952.5 %reduce-scatter.5.cloned.1.call-start = ((), (), s32[]{:S(2)}) async-start(), calls=%async_computation.8 | async-start | bytes 147456 | tf_op jit(solution)/shard_map/reduce_scatter | solution.py:166
  213.0 3.4 copy-start.11
  216.4 1.8 copy-start.12
  216.4 1.8 copy-start.15
  216.4 2.2 copy-start.16
  396.4 2.6 copy-start.6
  399.0 1.6 copy-start.8
  403.3 756.9 %reduce-scatter.3.cloned.1.call-start = ((), (), s32[]{:S(2)}) async-start(), calls=%async_computation.7 | async-start | bytes 2064384 | tf_op jit(solution)/shard_map/reduce_scatter | solution.py:165
  406.1 5.3 copy-start.7
  411.4 1.6 copy-start.5
  425.0 1.1 copy-start.4
  426.2 736.0 %copy-start.1 = (bf16[1,320,1792]{2,1,0:T(8,128)(2,1)S(1)}, bf16[1,320,1792]{2,1,0:T(8,128)(2,1)}, u32[]{:S(2)}) copy-start(bf16[1,320,1792]{2,1,0:T(8,128)(2,1)} %param.24) | copy-start | bytes 3440644
Sparse Core Ops, SparseCore 0:
  11.6 128.8 all-gather.8
  144.1 125.9 all-gather.10
  273.7 117.3 all-gather.6
  403.4 11.2 reduce-scatter.4
  426.3 31.4 reduce-scatter.2
where the time goes:
time: 1190 us; the launch traced here: 1170 us
  blocking collectives  731 us (61%)
  waiting for transfers between devices  251 us (21%)
  local copies, waits for them, and re-layouts  65.2 us (5%)
  starting transfers between devices  55.2 us (5%)
  matrix products  27.2 us (2%)
  other arithmetic  23.8 us (2%)
  between operations  15.4 us (1%)
    unnamed x1, blocking collectives  731 us
    all_gather x1, waiting for transfers between devices, local(): lax.all_gather(hot_down, 'dp', axis=0, tiled=True)  116 us
    all_to_all x1, waiting for transfers between devices, local(): lax.all_to_all(send_in, 'dp', split_axis=0, concat_axis=0, tiled=True)  46.1 us
    all_gather x1, waiting for transfers between devices, local(): lax.all_gather(hot_gate, 'dp', axis=0, tiled=True)  41.6 us
    all_to_all x1, waiting for transfers between devices, local(): lax.all_to_all(send_grad, 'dp', split_axis=0, concat_axis=0, tiled=True)  38.9 us
    unnamed x42, local copies, waits for them, and re-layouts  24.4 us
  transfers between devices with their start and end apart: 10, of which 6 were waited for; matrix products, arithmetic and copies ran while one was open for 9% of the time, Pallas kernels for 0%

commit v1 on v0

v1 whole, which is shorter than its diff:
```python
import jax
import jax.numpy as jnp
from jax import lax
from jax.experimental import pallas as pl
from jax.experimental.pallas import tpu as pltpu
from jax.sharding import PartitionSpec as P

NX, NY, NZ = 4, 2, 8
CHIPS = NX * NY * NZ
RING = NY * NZ
CAP = 4
HCAP = 48
SIDE = 128
UNIT = 5
MESH = pl.DeviceIdType.MESH
F32 = jnp.float32
BF16 = jnp.bfloat16
VMEM = pltpu.VMEM
ROWS = (((0,), (0,)), ((), ()))
COLS = (((1,), (1,)), ((), ()))


def spec(space):
    return pl.BlockSpec(memory_space=space)


def params(**more):
    return pltpu.CompilerParams(vmem_limit_bytes=56 << 20, **more)


def iota(shape, axis):
    return lax.broadcasted_iota(jnp.int32, shape, axis)


def positions_kernel(flags, owner, ids, slots, out):
    chosen = ids[...]
    count = flags.shape[0]

    def step(entry, carry):
        hot, place = carry
        same = chosen == entry
        hot = jnp.where(same, flags[entry], hot)
        place = jnp.where(same, owner[entry], place)
        return hot, place

    zero = jnp.zeros(chosen.shape, jnp.int32)
    hot, place = lax.fori_loop(0, count, step, (zero, zero))
    slot = slots[...]
    cold_row = jnp.where(slot < CAP, place * CAP + slot, -1)
    hot_row = jnp.where(slot < HCAP, CHIPS * CAP + slot, -1)
    out[...] = jnp.where(hot == 1, hot_row, cold_row)


def cold_match(pos, low, rows, token_count):
    row = low + iota((rows, token_count), 0)
    within = row & 7
    return row, within, (row >> 3) * CAP + (within & 3)


def pack_kernel(flags, owner, ids, slots, probs, tokens, grad, gate, up, down, cold, hot, weights, pos):
    positions_kernel(flags, owner, ids, slots, pos)
    token_count, width = tokens.shape
    block = 8 * min(CHIPS, 16)
    gates = probs[...].astype(F32)

    def step(index, carry):
        low = pl.multiple_of(index * block, block)
        row, within, want = cold_match(pos, low, block, token_count)
        first = pos[0:1, :] == want
        second = pos[1:2, :] == want
        match = first | second
        pick_x = jnp.where(match & (within < CAP), 1.0, 0.0).astype(BF16)
        pick_g = jnp.where(match & (within >= CAP), 1.0, 0.0).astype(BF16)
        rows = jnp.dot(pick_x, tokens[...], preferred_element_type=F32)
        rows += jnp.dot(pick_g, grad[...], preferred_element_type=F32)
        cold[pl.ds(low, block), :width] = rows.astype(BF16)
        scale = jnp.where(first, gates[0:1, :], 0.0) + jnp.where(second, gates[1:2, :], 0.0)
        scale = jnp.sum(scale, axis=1, keepdims=True)
        cold[pl.ds(low, block), width:] = jnp.broadcast_to(scale, (block, SIDE)).astype(BF16)
        return carry

    lax.fori_loop(0, 8 * CHIPS // block, step, 0)
    want = CHIPS * CAP + iota((HCAP, token_count), 0)
    first = pos[0:1, :] == want
    second = pos[1:2, :] == want
    pick = jnp.where(first | second, 1.0, 0.0).astype(BF16)
    hot[:HCAP, :width] = jnp.dot(pick, tokens[...], preferred_element_type=F32).astype(BF16)
    hot[HCAP:, :width] = jnp.dot(pick, grad[...], preferred_element_type=F32).astype(BF16)
    scale = jnp.where(first, gates[0:1, :], 0.0) + jnp.where(second, gates[1:2, :], 0.0)
    scale = jnp.broadcast_to(jnp.sum(scale, axis=1, keepdims=True), (HCAP, SIDE)).astype(BF16)
    hot[:HCAP, width:] = scale
    hot[HCAP:, width:] = scale
    rest = jnp.zeros((16 - 3 * UNIT, width), F32)
    parts = [gate[...].astype(F32), up[...].astype(F32), down[...].astype(F32), rest]
    weights[...] = jnp.concatenate(parts, axis=0).astype(BF16)


def place():
    me = lax.axis_index("dp")
    core = lax.rem(me, 2)
    chip = lax.div(me, 2)
    return me, lax.axis_index("pair"), core, chip, lax.div(chip, RING), lax.rem(chip, RING)


def ring_shift(at, k):
    y, z = lax.div(at, NZ), lax.rem(at, NZ)
    return lax.rem(y + lax.div(k, NZ), NY) * NZ + lax.rem(z + lax.rem(k, NZ), NZ)


def remote(src, dst, send, recv, dp, pair):
    return pltpu.make_async_remote_copy(
        src_ref=src, dst_ref=dst, send_sem=send, recv_sem=recv, device_id=(dp, pair), device_id_type=MESH
    )


def greet(pair, core, x, at, sibling):
    barrier = pltpu.get_barrier_semaphore()

    def each(k, carry):
        chip = lax.rem(x + lax.div(k, RING), NX) * RING + ring_shift(at, lax.rem(k, RING))
        pl.semaphore_signal(barrier, inc=1, device_id=(chip * 2 + core, pair), device_id_type=MESH)
        return carry

    lax.fori_loop(1, CHIPS, each, 0)
    pl.semaphore_signal(barrier, inc=1, device_id=(sibling, pair), device_id_type=MESH)
    pl.semaphore_wait(barrier, CHIPS)


def spread_kernel(cold_in, hot_in, w_in, cold, hot, w, own, cold_send, hot_send, w_send, cold_recv, hot_recv, w_recv, side_send, side_recv):
    me, pair, core, chip, x, at = place()
    sibling = me + 1 - 2 * core
    mine = [
        pltpu.make_async_copy(cold_in.at[chip], cold.at[core, chip], own.at[0]),
        pltpu.make_async_copy(hot_in, hot.at[core, x], own.at[1]),
        pltpu.make_async_copy(w_in, w.at[at], own.at[2]),
    ]
    for copy in mine:
        copy.start()
    greet(pair, core, x, at, sibling)

    def send_w(k, carry):
        other = ring_shift(at, k)
        remote(w_in, w.at[at], w_send, w_recv, (x * RING + other) * 2 + core, pair).start()
        return carry

    lax.fori_loop(1, RING, send_w, 0)
    for j in range(1, NX):
        other = lax.rem(x + j, NX)
        remote(hot_in, hot.at[core, x], hot_send, hot_recv, (other * RING + at) * 2 + core, pair).start()
    for j in range(NX):

        def send_cold(k, carry, j=j):
            other = lax.rem(x + j, NX) * RING + ring_shift(at, k)
            remote(cold_in.at[other], cold.at[core, chip], cold_send, cold_recv.at[j], other * 2 + core, pair).start()
            return carry

        lax.fori_loop(1 if j == 0 else 0, RING, send_cold, 0)
    for copy in mine:
        copy.wait()

    remote(hot.at[core, pl.ds(0, NX - 1)], hot.at[core, pl.ds(0, NX - 1)], hot_send, hot_recv, sibling, pair).wait_recv()
    forward = [remote(hot.at[core], hot.at[core], side_send.at[NX], side_recv.at[NX], sibling, pair)]
    forward[0].start()
    for j in range(NX):
        source = lax.rem(x + NX - j, NX) * RING
        got = cold.at[core, pl.ds(source, RING - 1 if j == 0 else RING)]
        remote(got, got, cold_send, cold_recv.at[j], sibling, pair).wait_recv()
        block = cold.at[core, pl.ds(source, RING)]
        forward.append(remote(block, block, side_send.at[j], side_recv.at[j], sibling, pair))
        forward[-1].start()
    for copy in forward:
        copy.wait()
    remote(w.at[pl.ds(0, RING - 1)], w.at[pl.ds(0, RING - 1)], w_send, w_recv, sibling, pair).wait()
    remote(hot.at[core, pl.ds(0, NX - 1)], hot.at[core, pl.ds(0, NX - 1)], hot_send, hot_recv, sibling, pair).wait_send()
    sent = cold_in.at[pl.ds(0, CHIPS - 1)]
    remote(sent, sent, cold_send, cold_recv.at[0], sibling, pair).wait_send()


def swish(pre_gate, pre_up, back, scale):
    sigmoid = 1.0 / (1.0 + jnp.exp(-pre_gate))
    act = pre_gate * sigmoid
    hidden = act * pre_up
    probs = hidden * back
    hidden_grad = scale * back
    gate_grad = hidden_grad * pre_up * sigmoid * (1.0 + pre_gate * (1.0 - sigmoid))
    return gate_grad, hidden_grad * act, scale * hidden, probs


def work_kernel(cold, hot, w, c_gate, c_up, c_down, cold_out, hot_out, w_out, g_gate, g_up, g_down, d_gate, d_up, d_down, h_gate, h_down):
    width = c_gate.shape[1]
    half = width // 2
    rows = cold.shape[0]
    block = min(rows, 256)

    def cold_step(index, carry):
        at = pl.ds(pl.multiple_of(index * block, block), block)
        data = cold[at, :width]
        scale = cold[at, width : width + SIDE].astype(F32)[:, :1]
        pre_gate = lax.dot_general(data, c_gate[...], COLS, preferred_element_type=F32)
        pre_up = lax.dot_general(data, c_up[...], COLS, preferred_element_type=F32)
        back = lax.dot_general(data, c_down[...], COLS, preferred_element_type=F32)
        back = pltpu.roll(back, block - CAP, 0)
        gate_grad, up_grad, weighted, probs = swish(pre_gate, pre_up, back, scale)
        is_x = (iota(pre_gate.shape, 0) & 7) < CAP
        gate_grad = jnp.where(is_x, gate_grad, 0.0).astype(BF16)
        up_grad = jnp.where(is_x, up_grad, 0.0).astype(BF16)
        d_gate[at, :] = gate_grad
        d_up[at, :] = up_grad
        d_down[at, :] = pltpu.roll(jnp.where(is_x, weighted, 0.0), CAP, 0).astype(BF16)
        dx = jnp.dot(gate_grad, c_gate[...], preferred_element_type=F32)
        dx += jnp.dot(up_grad, c_up[...], preferred_element_type=F32)
        is_x = (iota((block, half), 0) & 7) < CAP
        packed = jnp.where(is_x, dx[:, :half], pltpu.roll(dx[:, half:], CAP, 0))
        cold_out[at, :half] = packed.astype(BF16)
        probs = jnp.sum(probs, axis=1, keepdims=True)
        cold_out[at, half:] = jnp.broadcast_to(probs, (block, SIDE)).astype(BF16)
        return carry

    lax.fori_loop(0, rows // block, cold_step, 0)
    step = 256
    for grads, out in ((d_gate, g_gate), (d_up, g_up), (d_down, g_down)):

        def grad_step(index, carry, grads=grads, out=out):
            at = pl.ds(pl.multiple_of(index * step, step), step)
            out[:, at] = lax.dot_general(grads[...], cold[:, at], ROWS, preferred_element_type=F32).astype(BF16)
            return carry

        lax.fori_loop(0, width // step, grad_step, 0)

    units = w.shape[0]
    lane = iota((HCAP, units), 1) & 15

    def hot_step(index, carry):
        both = pl.multiple_of(index * 2 * HCAP, 2 * HCAP)
        at = pl.ds(pl.multiple_of(index * HCAP, HCAP), HCAP)
        rows_in = hot[pl.ds(both, HCAP), :width]
        rows_grad = hot[pl.ds(both + HCAP, HCAP), :width]
        scale = hot[pl.ds(both, HCAP), width : width + SIDE].astype(F32)[:, :1]
        pre = lax.dot_general(rows_in, w[...], COLS, preferred_element_type=F32)
        back = lax.dot_general(rows_grad, w[...], COLS, preferred_element_type=F32)
        pre_up = pltpu.roll(pre, units - UNIT, 1)
        back = pltpu.roll(back, units - 2 * UNIT, 1)
        gate_grad, up_grad, weighted, probs = swish(pre, pre_up, back, scale)
        live = lane < UNIT
        up_grad = pltpu.roll(jnp.where(live, up_grad, 0.0), UNIT, 1)
        grads = (jnp.where(live, gate_grad, 0.0) + up_grad).astype(BF16)
        h_gate[pl.ds(both, HCAP), :] = grads
        h_gate[pl.ds(both + HCAP, HCAP), :] = pltpu.roll(jnp.where(live, weighted, 0.0), 2 * UNIT, 1).astype(BF16)
        hot_out[at, :width] = jnp.dot(grads, w[...], preferred_element_type=F32).astype(BF16)
        probs = jnp.sum(jnp.where(live, probs, 0.0), axis=1, keepdims=True)
        hot_out[at, width:] = jnp.broadcast_to(probs, (HCAP, SIDE)).astype(BF16)
        return carry

    lax.fori_loop(0, 2 * NX, hot_step, 0)

    def hot_grad_step(index, carry):
        at = pl.ds(pl.multiple_of(index * step, step), step)
        w_out[:, at] = lax.dot_general(h_gate[...], hot[:, at], ROWS, preferred_element_type=F32).astype(BF16)
        return carry

    lax.fori_loop(0, width // step, hot_grad_step, 0)


def collect_kernel(cold_in, hot_in, w_in, cold, hot, w, side_cold, side_hot, sum_cold, sum_hot, own, cold_send, hot_send, w_send, cold_recv, hot_recv, w_recv, side_send, side_recv):
    me, pair, core, chip, x, at = place()
    sibling = me + 1 - 2 * core
    keep = pltpu.make_async_copy(w_in.at[at], w.at[at], own.at[0])
    keep.start()
    greet(pair, core, x, at, sibling)
    aside = [remote(hot_in.at[1 - core], side_hot, side_send.at[NX], side_recv.at[NX], sibling, pair)]
    for j in range(NX):
        block = pl.ds(lax.rem(x + j, NX) * RING, RING)
        aside.append(remote(cold_in.at[1 - core, block], side_cold.at[block], side_send.at[j], side_recv.at[j], sibling, pair))
    for copy in aside:
        copy.start()

    def send_w(k, carry):
        other = ring_shift(at, k)
        remote(w_in.at[other], w.at[at], w_send, w_recv, (x * RING + other) * 2 + core, pair).start()
        return carry

    lax.fori_loop(1, RING, send_w, 0)

    aside[0].wait_recv()

    def add_hot(k, carry):
        sum_hot[k] = (hot_in[core, k].astype(F32) + side_hot[k].astype(F32)).astype(BF16)
        return carry

    lax.fori_loop(0, NX, add_hot, 0)
    for j in range(1, NX):
        other = lax.rem(x + j, NX)
        remote(sum_hot.at[other], hot.at[x], hot_send, hot_recv, (other * RING + at) * 2 + core, pair).start()
    mine = [pltpu.make_async_copy(sum_hot.at[x], hot.at[x], own.at[1])]
    mine[0].start()
    for j in range(NX):
        base = lax.rem(x + j, NX) * RING
        aside[1 + j].wait_recv()

        def add_cold(k, carry, base=base):
            other = base + k
            sum_cold[other] = (cold_in[core, other].astype(F32) + side_cold[other].astype(F32)).astype(BF16)
            return carry

        lax.fori_loop(0, RING, add_cold, 0)

        def send_cold(k, carry, base=base):
            other = base + ring_shift(at, k)
            remote(sum_cold.at[other], cold.at[chip], cold_send, cold_recv, other * 2 + core, pair).start()
            return carry

        lax.fori_loop(1 if j == 0 else 0, RING, send_cold, 0)
        if j == 0:
            mine.append(pltpu.make_async_copy(sum_cold.at[chip], cold.at[chip], own.at[2]))
            mine[1].start()
    for copy in aside:
        copy.wait_send()
    keep.wait()
    for copy in mine:
        copy.wait()
    for ref, send, recv, count in ((w, w_send, w_recv, RING - 1), (hot, hot_send, hot_recv, NX - 1), (cold, cold_send, cold_recv, CHIPS - 1)):
        part = ref.at[pl.ds(0, count)]
        remote(part, part, send, recv, sibling, pair).wait()


def unpack_kernel(pos, cold, hot, w, own_rows, other_rows, probs, g_gate, g_up, g_down, total):
    token_count = pos.shape[1]
    half = cold.shape[1] - SIDE
    width = 2 * half
    rows = cold.shape[0]
    mine = token_count // 2
    pair = lax.axis_index("pair")
    row, within, want = cold_match(pos, 0, rows, token_count)
    first = pos[0:1, :] == want
    second = pos[1:2, :] == want
    match = first | second
    pick_low = jnp.where(match & (within < CAP), 1.0, 0.0).astype(BF16)
    pick_high = jnp.where(match & (within >= CAP), 1.0, 0.0).astype(BF16)
    hot_rows = hot.shape[0]
    hot_want = CHIPS * CAP + lax.rem(iota((hot_rows, token_count), 0), HCAP)
    hot_first = pos[0:1, :] == hot_want
    hot_second = pos[1:2, :] == hot_want
    pick_hot = jnp.where(hot_first | hot_second, 1.0, 0.0).astype(BF16)
    for low, pick in ((0, pick_low), (half, pick_high)):
        part = lax.dot_general(pick, cold[:, :half], ROWS, preferred_element_type=F32)
        part += lax.dot_general(pick_hot, hot[:, low : low + half], ROWS, preferred_element_type=F32)
        total[:, low : low + half] = part
    own_rows[...] = total[pl.ds(pl.multiple_of(pair * mine, 8), mine), :]
    other_rows[...] = total[pl.ds(pl.multiple_of((1 - pair) * mine, 8), mine), :].astype(BF16)
    cold_probs = cold[:, half:].astype(F32)[:, :1]
    hot_probs = hot[:, width:].astype(F32)[:, :1]
    is_x = within < CAP
    for k, (a, b) in enumerate(((first, hot_first), (second, hot_second))):
        value = jnp.sum(jnp.where(a & is_x, cold_probs, 0.0), axis=0, keepdims=True)
        value += jnp.sum(jnp.where(b, hot_probs, 0.0), axis=0, keepdims=True)
        probs[k : k + 1, :] = value
    grads = w[0].astype(F32)
    for k in range(1, w.shape[0]):
        grads += w[k].astype(F32)
    g_gate[...] = grads[0:UNIT].astype(BF16)
    g_up[...] = grads[UNIT : 2 * UNIT].astype(BF16)
    g_down[...] = grads[2 * UNIT : 3 * UNIT].astype(BF16)


def shape(*dims, dtype=BF16):
    return jax.ShapeDtypeStruct(dims, dtype)


def local(tokens, grad_out, gate_probs, expert_ids, route_slots, hot_flags, owner_slot, cold_gate, cold_up, cold_down, hot_gate, hot_up, hot_down):
    token_count, width = tokens.shape
    wide, half = width + SIDE, width // 2
    ff = cold_gate.shape[1]
    units = 16 * RING
    dma = pltpu.SemaphoreType.DMA
    cold, hot, weights, pos = pl.pallas_call(
        pack_kernel,
        out_shape=(shape(8 * CHIPS, wide), shape(2 * HCAP, wide), shape(16, width), shape(2, token_count, dtype=jnp.int32)),
        in_specs=[spec(pltpu.SMEM)] * 2 + [spec(VMEM)] * 8,
        out_specs=[spec(VMEM)] * 4,
        compiler_params=params(),
    )(hot_flags, owner_slot, expert_ids.T, route_slots.T, gate_probs.T, tokens, grad_out, hot_gate, hot_up, hot_down)

    got_cold, got_hot, got_w = pl.pallas_call(
        spread_kernel,
        out_shape=(shape(2, CHIPS, 8, wide), shape(2, NX, 2 * HCAP, wide), shape(RING, 16, width)),
        in_specs=[spec(pl.ANY)] * 3,
        out_specs=[spec(pl.ANY)] * 3,
        scratch_shapes=[dma((3,)), dma, dma, dma, dma((NX,)), dma, dma, dma((NX + 1,)), dma((NX + 1,))],
        compiler_params=params(collective_id=0, has_side_effects=True),
    )(cold.reshape(CHIPS, 8, wide), hot, weights)

    ret_cold, ret_hot, ret_w, g_gate, g_up, g_down = pl.pallas_call(
        work_kernel,
        out_shape=(shape(16 * CHIPS, half + SIDE), shape(2 * NX * HCAP, wide), shape(units, width)) + (shape(ff, width),) * 3,
        in_specs=[spec(VMEM)] * 6,
        out_specs=[spec(VMEM)] * 6,
        scratch_shapes=[VMEM((16 * CHIPS, ff), BF16)] * 3 + [VMEM((4 * NX * HCAP, units), BF16)] * 2,
        compiler_params=params(),
    )(got_cold.reshape(16 * CHIPS, wide), got_hot.reshape(4 * NX * HCAP, wide), got_w.reshape(units, width), cold_gate[0], cold_up[0], cold_down[0])

    back_cold, back_hot, back_w = pl.pallas_call(
        collect_kernel,
        out_shape=(shape(CHIPS, 8, half + SIDE), shape(NX, HCAP, wide), shape(RING, 16, width)),
        in_specs=[spec(VMEM), spec(VMEM), spec(pl.ANY)],
        out_specs=[spec(pl.ANY)] * 3,
        scratch_shapes=[
            VMEM((CHIPS, 8, half + SIDE), BF16),
            VMEM((NX, HCAP, wide), BF16),
            VMEM((CHIPS, 8, half + SIDE), BF16),
            VMEM((NX, HCAP, wide), BF16),
            dma((3,)), dma, dma, dma, dma, dma, dma, dma((NX + 1,)), dma((NX + 1,)),
        ],
        compiler_params=params(collective_id=1, has_side_effects=True),
    )(ret_cold.reshape(2, CHIPS, 8, half + SIDE), ret_hot.reshape(2, NX, HCAP, wide), ret_w.reshape(RING, 16, width))

    mine = token_count // 2
    own_rows, other_rows, probs, h_gate, h_up, h_down = pl.pallas_call(
        unpack_kernel,
        out_shape=(shape(mine, width, dtype=F32), shape(mine, width), shape(2, token_count, dtype=F32)) + (shape(UNIT, width),) * 3,
        in_specs=[spec(VMEM)] * 4,
        out_specs=[spec(VMEM)] * 6,
        scratch_shapes=[VMEM((token_count, width), F32)],
        compiler_params=params(),
    )(pos, back_cold.reshape(8 * CHIPS, half + SIDE), back_hot.reshape(NX * HCAP, wide), back_w)

    swap = [(0, 1), (1, 0)]
    pair = lax.axis_index("pair")
    halves = probs.T.reshape(2, mine, 2)
    own_probs = jnp.where(pair == 0, halves[0], halves[1])
    other_probs = jnp.where(pair == 0, halves[1], halves[0])
    summed = own_rows + lax.ppermute(other_rows, "pair", swap).astype(F32)
    summed_probs = own_probs + lax.ppermute(other_probs, "pair", swap)
    return (summed.astype(BF16), summed_probs, g_gate[None], g_up[None], g_down[None], h_gate, h_up, h_down)


def solution(mesh):
    split = P(("dp", "pair"), None)
    cold = P("dp", "pair", None)
    return jax.shard_map(
        local,
        mesh=mesh,
        in_specs=(P("dp", None),) * 5 + (P(), P()) + (cold,) * 3 + (split,) * 3,
        out_specs=(split, split, cold, cold, cold, split, split, split),
        check_vma=False,
    )
```

time: 1190 us -> 196 us (0.16); the launches traced: 1170 us -> 196 us
  blocking collectives: 731 us -> 0 us
  waiting for transfers between devices: 251 us -> 6.55 us
  Pallas kernels: 0 us -> 183 us
  local copies, waits for them, and re-layouts: 65.2 us -> 0 us
  starting transfers between devices: 55.2 us -> 1.47 us
  matrix products: 27.2 us -> 0 us
  other arithmetic: 23.8 us -> 4.08 us
  between operations: 15.4 us -> 0.66 us
    unnamed x1 -> x0, blocking collectives: 731 us -> none
    pallas_call x0 -> x5, Pallas kernels: none -> 183 us  [the longest x1 81.3 us: local(): pl.pallas_call(spread_kernel, out_shape=(shape(2, CHIPS, 8, wide), shape(...]
    all_gather x3 -> x0, waiting for transfers between devices: 157 us -> none  [the longest x1 116 us: local(): lax.all_gather(hot_down, 'dp', axis=0, tiled=True)]
    all_to_all x5 -> x0, waiting for transfers between devices: 92 us -> none  [the longest x1 46.1 us: local(): lax.all_to_all(send_in, 'dp', split_axis=0, concat_axis=0, tiled=True)]
    all_to_all x5 -> x0, starting transfers between devices: 54.7 us -> none  [the longest x1 16.4 us: local(): lax.all_to_all(send_gate, 'dp', split_axis=0, concat_axis=0, tiled=True)]
    dot_general x16 -> x0, matrix products: 27.2 us -> none  [the longest x2 6.15 us: expert_back(): pre_up = jnp.dot(rows_in, w_up.T, preferred_element_type=jnp.float32)]
    unnamed x42 -> x0, local copies, waits for them, and re-layouts: 24.4 us -> none
    reshape x8 -> x0, local copies, waits for them, and re-layouts: 16 us -> none  [the longest x1 5.06 us: local(): owner_dx.reshape(device_count, CAP, model_width)]
  transfers between devices with their start and end apart: 10 -> 2, of which waited for: 6 -> 1; matrix products, arithmetic and copies ran while one was open for 9% -> 1% of each run, Pallas kernels for 0% -> 0%
where the time goes in v1:
time: 196 us
  Pallas kernels  183 us (93%)
  waiting for transfers between devices  6.55 us (3%)
  other arithmetic  4.08 us (2%)
    pallas_call x1, Pallas kernels, local(): pl.pallas_call(spread_kernel, out_shape=(shape(2, CHIPS, 8, wide), shape(...  81.3 us
    pallas_call x1, Pallas kernels, local(): pl.pallas_call(collect_kernel, out_shape=(shape(CHIPS, 8, half + SIDE), s...  55.2 us
    pallas_call x1, Pallas kernels, local(): pl.pallas_call(work_kernel, out_shape=(shape(16 * CHIPS, half + SIDE), sh...  37.9 us
    ppermute x1, waiting for transfers between devices, local(): summed_probs = own_probs + lax.ppermute(other_probs, 'pair', swap)  6.55 us
    pallas_call x1, Pallas kernels, local(): pl.pallas_call(pack_kernel, out_shape=(shape(8 * CHIPS, wide), shape(2 *...  4.76 us
  transfers between devices with their start and end apart: 2, of which 1 were waited for; matrix products, arithmetic and copies ran while one was open for 1% of the time, Pallas kernels for 0%

profile of v1, /device:TPU:1, one launch (start us, length us, event | category | flops | bytes accessed | tf_op | source)
XLA Modules:
  0.0 195.8 jit_solution(16356505870056830859)
XLA Ops:
  0.6 4.8 %shard_map.188 = (bf16[512,1920]{1,0:T(8,128)(2,1)}, bf16[96,1920]{1,0:T(8,128)(2,1)}, bf16[16,1792]{1,0:T(8,128)(2,1)}, s32[2,192]{1,0:T(2,128)}) custom-call(s32[65]{0:T(128)} %flags.1, s32[65]{0:T(128)} %owner.1, s32[2,192]{1,0:T(2,128)} %bitcast.33, s32[2,192]{1,0:T(2,128)} %bitcast.34, bf16[2,192]{1,0:T(2,128)(2,1)} %bitcast.35, ...), custom_call_target="tpu_custom_call" | custom-call | tf_op jit(solution)/shard_map/pallas_call | solution.py:375
  5.4 81.3 %shard_map.189 = (bf16[2,64,8,1920]{3,2,1,0:T(8,128)(2,1)}, bf16[2,4,96,1920]{3,2,1,0:T(8,128)(2,1)}, bf16[16,16,1792]{2,1,0:T(8,128)(2,1)}) custom-call(bf16[64,8,1920]{2,1,0:T(8,128)(2,1)} %bitcast.22, bf16[96,1920]{1,0:T(8,128)(2,1)} %get-tuple-element.32.hot_in, bf16[16,1792]{1,0:T(8,128)(2,1)} %get-tuple-element.33.w_in), custom_call_target="tpu_custom_call" | custom-call | tf_op jit(solution)/shard_map/pallas_call | solution.py:383
  86.7 37.9 %shard_map.190 = (bf16[1024,1024]{1,0:T(8,128)(2,1)}, bf16[384,1920]{1,0:T(8,128)(2,1)}, bf16[256,1792]{1,0:T(8,128)(2,1)}, bf16[320,1792]{1,0:T(8,128)(2,1)}, b...) custom-call(bf16[1024,1920]{1,0:T(8,128)(2,1)} %bitcast.19, bf16[768,1920]{1,0:T(8,128)(2,1)} %bitcast.20, ...), custom_call_target="tpu_custom_call" | custom-call | tf_op jit(solution)/shard_map/pallas_call | solution.py:392
  124.6 55.2 %shard_map.191 = (bf16[64,8,1024]{2,1,0:T(8,128)(2,1)}, bf16[4,48,1920]{2,1,0:T(8,128)(2,1)}, bf16[16,16,1792]{2,1,0:T(8,128)(2,1)}) custom-call(bf16[2,64,8,1024]{3,2,1,0:T(8,128)(2,1)} %bitcast.21, bf16[2,4,48,1920]{3,2,1,0:T(8,128)(2,1)} %bitcast.23, bf16[16,16,1792]{2,1,0:T(8,128)(2,1)} %bitcast.29), custom_call_target="tpu_custom_call" | custom-call | tf_op jit(solution)/shard_map/pallas_call | solution.py:401
  179.8 3.9 %shard_map.192 = (f32[96,1792]{1,0:T(8,128)}, bf16[96,1792]{1,0:T(8,128)(2,1)}, f32[2,192]{1,0:T(2,128)}, bf16[5,1792]{1,0:T(8,128)(2,1)}, bf16[5,1792]{1,0:T(8,128)(2,1)}, /*index=5*/bf16[5,1792]{1,0:T(8,128)(2,1)}) custom-call(s32[2,192]{1,0:T(2,128)} %get-tuple-element.30.pos, bf16[512,1024]{1,0:T(8,128)(2,1)} %bitcast.27, bf16[192,1920]{1,0:T(8,128)(2,1)} %bitcast.30, ...), custom_call_target="tpu_custom_call" | custom-call | tf_op jit(solution)/shard_map/pallas_call | solution.py:417
  183.7 1.2 collective-permute-start
  184.9 0.8 broadcast_select_fusion
  185.7 0.3 collective-permute-start.1
  186.0 6.5 %collective-permute-done.1 = f32[96,2]{0,1:T(2,128)S(1)} collective-permute-done((f32[96,2]{0,1:T(2,128)S(1)}, f32[96,2]{0,1:T(2,128)S(1)}, u32[]{:S(2)}, u32[]{:S(2)}) %collective-permute-start.1) | collective-permute-done | bytes 800 | tf_op jit(solution)/shard_map/ppermute | solution.py:432
  192.5 1.4 select_add_fusion
  193.9 0.0 collective-permute-done
  193.9 1.9 add_convert_fusion
Async XLA Ops:
  183.7 10.2 %collective-permute-start = (bf16[96,1792]{1,0:T(8,128)(2,1)}, bf16[96,1792]{1,0:T(8,128)(2,1)S(1)}, u32[]{:S(2)}, u32[]{:S(2)}) collective-permute-start(bf16[96,1792]{1,0:T(8,128)(2,1)} %get-tuple-element.44), channel_id=1, source_target_pairs={{0,1},{1,0},{2,3},{3,2},{4,5},{5,4},{6,7},{7,6},{8,9},{9,8},{10,11... | collective-permute-start | bytes 1032200 | tf_op jit(solution)/shard_map/ppermute | solution.py:431
  185.7 6.8 %collective-permute-start.1 = (f32[96,2]{0,1:T(2,128)S(1)}, f32[96,2]{0,1:T(2,128)S(1)}, u32[]{:S(2)}, u32[]{:S(2)}) collective-permute-start(f32[96,2]{0,1:T(2,128)S(1)} %broadcast_select_fusion), channel_id=1, source_target_pairs={{0,1},{1,0},{2,3},{3,2},{4,5},{5,4},{6,7},{7,6},{8,9},{9,8},{10,11... | collective-permute-start | bytes 2312 | tf_op jit(solution)/shard_map/ppermute | solution.py:432

commit v2 on v1

v2 whole, which is shorter than its diff:
```python
import jax
import jax.numpy as jnp
from jax import lax
from jax.experimental import pallas as pl
from jax.experimental.pallas import tpu as pltpu
from jax.sharding import PartitionSpec as P

NX, NY, NZ = 4, 2, 8
CHIPS = NX * NY * NZ
RING = NY * NZ
CAP = 4
HCAP = 48
SIDE = 128
UNIT = 5
GROUPS = NX * NY // 2
MESH = pl.DeviceIdType.MESH
F32 = jnp.float32
BF16 = jnp.bfloat16
VMEM = pltpu.VMEM
ROWS = (((0,), (0,)), ((), ()))
COLS = (((1,), (1,)), ((), ()))


def spec(space):
    return pl.BlockSpec(memory_space=space)


def params(**more):
    return pltpu.CompilerParams(vmem_limit_bytes=56 << 20, **more)


def iota(shape, axis):
    return lax.broadcasted_iota(jnp.int32, shape, axis)


def positions_kernel(flags, owner, ids, slots, out):
    chosen = ids[...]
    count = flags.shape[0]

    def step(entry, carry):
        hot, place = carry
        same = chosen == entry
        hot = jnp.where(same, flags[entry], hot)
        place = jnp.where(same, owner[entry], place)
        return hot, place

    zero = jnp.zeros(chosen.shape, jnp.int32)
    hot, place = lax.fori_loop(0, count, step, (zero, zero))
    slot = slots[...]
    cold_row = jnp.where(slot < CAP, place * CAP + slot, -1)
    hot_row = jnp.where(slot < HCAP, CHIPS * CAP + slot, -1)
    out[...] = jnp.where(hot == 1, hot_row, cold_row)


def cold_match(pos, low, rows, token_count):
    row = low + iota((rows, token_count), 0)
    within = row & 7
    return row, within, (row >> 3) * CAP + (within & 3)


def pack_kernel(flags, owner, ids, slots, probs, tokens, grad, gate, up, down, cold, hot_x, hot_g, weights, pos):
    positions_kernel(flags, owner, ids, slots, pos)
    token_count, width = tokens.shape
    block = 8 * min(CHIPS, 16)
    gates = probs[...].astype(F32)

    def step(index, carry):
        low = pl.multiple_of(index * block, block)
        row, within, want = cold_match(pos, low, block, token_count)
        first = pos[0:1, :] == want
        second = pos[1:2, :] == want
        match = first | second
        pick_x = jnp.where(match & (within < CAP), 1.0, 0.0).astype(BF16)
        pick_g = jnp.where(match & (within >= CAP), 1.0, 0.0).astype(BF16)
        rows = jnp.dot(pick_x, tokens[...], preferred_element_type=F32)
        rows += jnp.dot(pick_g, grad[...], preferred_element_type=F32)
        cold[pl.ds(low, block), :width] = rows.astype(BF16)
        scale = jnp.where(first, gates[0:1, :], 0.0) + jnp.where(second, gates[1:2, :], 0.0)
        scale = jnp.sum(scale, axis=1, keepdims=True)
        cold[pl.ds(low, block), width:] = jnp.broadcast_to(scale, (block, SIDE)).astype(BF16)
        return carry

    lax.fori_loop(0, 8 * CHIPS // block, step, 0)
    want = CHIPS * CAP + iota((HCAP, token_count), 0)
    first = pos[0:1, :] == want
    second = pos[1:2, :] == want
    pick = jnp.where(first | second, 1.0, 0.0).astype(BF16)
    hot_x[:, :width] = jnp.dot(pick, tokens[...], preferred_element_type=F32).astype(BF16)
    hot_g[...] = jnp.dot(pick, grad[...], preferred_element_type=F32).astype(BF16)
    scale = jnp.where(first, gates[0:1, :], 0.0) + jnp.where(second, gates[1:2, :], 0.0)
    hot_x[:, width:] = jnp.broadcast_to(jnp.sum(scale, axis=1, keepdims=True), (HCAP, SIDE)).astype(BF16)
    rest = jnp.zeros((16 - 3 * UNIT, width), F32)
    parts = [gate[...].astype(F32), up[...].astype(F32), down[...].astype(F32), rest]
    weights[...] = jnp.concatenate(parts, axis=0).astype(BF16)


def place():
    me = lax.axis_index("dp")
    core = lax.rem(me, 2)
    chip = lax.div(me, 2)
    ring = lax.rem(chip, RING)
    return lax.axis_index("pair"), core, lax.div(chip, RING), lax.div(ring, NZ), lax.rem(ring, NZ)


def device(x, y, z, core, pair):
    return (((x * NY + y) * NZ + z) * 2 + core, pair)


def remote(src, dst, send, recv, to):
    return pltpu.make_async_remote_copy(
        src_ref=src, dst_ref=dst, send_sem=send, recv_sem=recv, device_id=to, device_id_type=MESH
    )


def swish(pre_gate, pre_up, back, scale):
    sigmoid = 1.0 / (1.0 + jnp.exp(-pre_gate))
    act = pre_gate * sigmoid
    hidden = act * pre_up
    probs = hidden * back
    hidden_grad = scale * back
    gate_grad = hidden_grad * pre_up * sigmoid * (1.0 + pre_gate * (1.0 - sigmoid))
    return gate_grad, hidden_grad * act, scale * hidden, probs


def layer_kernel(
    cold_in, hot_x_in, hot_g_in, w_in, c_gate, c_up, c_down,
    back_cold, back_hot, back_w, g_gate, g_up, g_down,
    cold, hot_x, hot_g, w, d_gate, d_up, d_down, d_hot, ret, away, side, pass_on, passed, final,
    hot_ret, hot_away, hot_side, hot_sum, w_ret,
    own, cold_send, cold_recv, hot_send, hot_recv, w_send, w_recv, near_send, near_recv, over_send, over_recv,
    side_send, side_recv, pass_send, pass_recv, back_send, back_recv, hb_send, hb_recv, wb_send, wb_recv, one_send,
):
    width = c_gate.shape[1]
    half = width // 2
    pair, core, x, y, z = place()
    sibling = device(x, y, z, 1 - core, pair)
    partner = device(x, y, z, core, 1 - pair)

    def along(kx, ky, kz):
        other_y = lax.rem(y + ky, NY)
        other_pair = lax.rem(pair + ky, 2)
        return device(lax.rem(x + kx, NX), other_y, lax.rem(z + kz, NZ), core, other_pair)

    barrier = pltpu.get_barrier_semaphore()

    def greet(k, carry):
        to = along(lax.div(k, RING), lax.div(lax.rem(k, RING), NZ), lax.rem(k, NZ))
        pl.semaphore_signal(barrier, inc=1, device_id=to, device_id_type=MESH)
        return carry

    lax.fori_loop(1, CHIPS, greet, 0)
    pl.semaphore_signal(barrier, inc=1, device_id=sibling, device_id_type=MESH)
    pl.semaphore_signal(barrier, inc=1, device_id=partner, device_id_type=MESH)
    pl.semaphore_wait(barrier, CHIPS + 1)

    def hot_at(which, k):
        return pl.ds(pl.multiple_of((which * NX + k) * HCAP, HCAP), HCAP)

    mine = [
        pltpu.make_async_copy(hot_x_in, hot_x.at[hot_at(core, 0)], own.at[0]),
        pltpu.make_async_copy(hot_g_in, hot_g.at[hot_at(core, 0)], own.at[1]),
        pltpu.make_async_copy(w_in, w.at[pl.ds(0, 16)], own.at[2]),
    ]
    for copy in mine:
        copy.start()
    for k in range(1, NX):
        remote(hot_x_in, hot_x.at[hot_at(core, k)], hot_send.at[0], hot_recv.at[0], along(k, 0, 0)).start()
        remote(hot_g_in, hot_g.at[hot_at(core, k)], hot_send.at[1], hot_recv.at[1], along(k, 0, 0)).start()

    def send_w(k, carry):
        slot = pl.ds(pl.multiple_of(k * 16, 16), 16)
        remote(w_in, w.at[slot], w_send, w_recv, along(0, lax.div(k, NZ), lax.rem(k, NZ))).start()
        return carry

    lax.fori_loop(1, RING, send_w, 0)

    def cold_at(group, which):
        return pl.ds((group * 2 + which) * NZ, NZ)

    for j in range(GROUPS):
        kx, ky = pair + 2 * (j // NY), j % NY
        to_x, to_y = lax.rem(x + kx, NX), lax.rem(y + ky, NY)

        def cold_copy(kz, j=j, kx=kx, ky=ky, to_x=to_x, to_y=to_y):
            chip = (to_x * NY + to_y) * NZ + lax.rem(z + kz, NZ)
            slot = (j * 2 + core) * NZ + z
            return cold_in.at[chip], cold.at[slot], along(kx, ky, kz)

        if j == 0:
            src, dst, to = cold_copy(0)

            @pl.when(pair == 0)
            def _():
                pltpu.make_async_copy(src, dst, cold_recv.at[0]).start()

            @pl.when(pair == 1)
            def _():
                remote(src, dst, one_send.at[0], cold_recv.at[0], to).start()

        def send_cold(kz, carry, j=j, cold_copy=cold_copy):
            src, dst, to = cold_copy(kz)
            remote(src, dst, cold_send, cold_recv.at[j], to).start()
            return carry

        lax.fori_loop(1 if j == 0 else 0, NZ, send_cold, 0)

    started = []

    def start(copy):
        copy.start()
        started.append(copy)
        return copy

    mine[0].wait()
    mine[1].wait()
    others = pl.ds(0, (NX - 1) * HCAP)
    remote(hot_x.at[others], hot_x.at[others], hot_send.at[0], hot_recv.at[0], sibling).wait_recv()
    remote(hot_g.at[others], hot_g.at[others], hot_send.at[1], hot_recv.at[1], sibling).wait_recv()
    this = pl.ds(pl.multiple_of(core * NX * HCAP, HCAP), NX * HCAP)
    hot_over = [
        start(remote(hot_x.at[this], hot_x.at[this], over_send.at[2 * GROUPS], over_recv.at[2 * GROUPS], sibling)),
        start(remote(hot_g.at[this], hot_g.at[this], over_send.at[2 * GROUPS + 1], over_recv.at[2 * GROUPS + 1], sibling)),
    ]
    mine[2].wait()
    w_others = pl.ds(0, (RING - 1) * 16)
    remote(w.at[w_others], w.at[w_others], w_send, w_recv, sibling).wait_recv()
    for copy in hot_over:
        copy.wait_recv()

    units = w.shape[0]
    hot_rows = hot_x.shape[0]
    lane = iota((hot_rows, units), 1) & 15
    scale = hot_x[:, width : width + SIDE].astype(F32)[:, :1]
    pre = lax.dot_general(hot_x[:, :width], w[...], COLS, preferred_element_type=F32)
    project = lax.dot_general(hot_g[...], w[...], COLS, preferred_element_type=F32)
    pre_up = pltpu.roll(pre, units - UNIT, 1)
    project = pltpu.roll(project, units - 2 * UNIT, 1)
    gate_grad, up_grad, weighted, probs = swish(pre, pre_up, project, scale)
    live = lane < UNIT
    up_grad = pltpu.roll(jnp.where(live, up_grad, 0.0), UNIT, 1)
    grads = (jnp.where(live, gate_grad, 0.0) + up_grad).astype(BF16)
    d_hot[:hot_rows, :] = grads
    d_hot[hot_rows:, :] = pltpu.roll(jnp.where(live, weighted, 0.0), 2 * UNIT, 1).astype(BF16)
    hot_ret[:, :width] = jnp.dot(grads, w[...], preferred_element_type=F32)
    probs = jnp.sum(jnp.where(live, probs, 0.0), axis=1, keepdims=True)
    hot_ret[:, width:] = jnp.broadcast_to(probs, (hot_rows, SIDE))
    that = pl.ds(pl.multiple_of((1 - core) * NX * HCAP, HCAP), NX * HCAP)
    hot_away[...] = hot_ret[that, :].astype(BF16)
    hot_swap = start(remote(hot_away, hot_side, side_send.at[2 * GROUPS], side_recv.at[2 * GROUPS], sibling))
    w_grad = lax.dot_general(d_hot[:hot_rows, :], hot_x[:, :width], ROWS, preferred_element_type=F32)
    w_grad += lax.dot_general(d_hot[hot_rows:, :], hot_g[...], ROWS, preferred_element_type=F32)
    w_ret[...] = w_grad.astype(BF16)

    def back(kx, ky, kz):
        return along(lax.rem(NX - kx, NX), ky, NZ - kz)

    def return_w(k, carry):
        slot = pl.ds(pl.multiple_of(k * 16, 16), 16)
        to = back(0, lax.div(k, NZ), lax.rem(k, NZ))
        remote(w_ret.at[slot], back_w.at[k], wb_send, wb_recv, to).start()
        return carry

    lax.fori_loop(1, RING, return_w, 0)
    mine = [pltpu.make_async_copy(w_ret.at[pl.ds(0, 16)], back_w.at[0], own.at[0])]
    mine[0].start()

    near, over = [], []

    def hand_over(group):
        ref = cold.at[cold_at(group, core)]
        over.append(start(remote(ref, ref, over_send.at[group], over_recv.at[group], sibling)))

    for j in range(GROUPS):
        ref = cold.at[cold_at(j, core)]
        remote(ref, ref, cold_send, cold_recv.at[j], sibling).wait_recv()
        to = cold.at[cold_at(GROUPS + j, core)]
        near.append(start(remote(ref, to, near_send.at[j], near_recv.at[j], partner)))
        hand_over(j)
    hot_swap.wait_recv()
    for k in range(NX):
        at = pl.ds(k * HCAP, HCAP)
        source = pl.ds(pl.multiple_of((core * NX + k) * HCAP, HCAP), HCAP)
        hot_sum[at, :] = (hot_ret[source, :] + hot_side[at, :].astype(F32)).astype(BF16)
        if k:
            remote(hot_sum.at[at], back_hot.at[k], hb_send, hb_recv, back(k, 0, 0)).start()
        else:
            mine.append(pltpu.make_async_copy(hot_sum.at[at], back_hot.at[0], own.at[1]))
            mine[1].start()
    for j in range(GROUPS):
        near[j].wait_recv()
        hand_over(GROUPS + j)

    block = 4 * 8 * NZ
    side_copies = {}

    def compute(index):
        for group in (2 * index, 2 * index + 1):
            over[group].wait_recv()
        at = slice(index * block, (index + 1) * block)
        data = cold[index * 4 * NZ : (index + 1) * 4 * NZ].reshape(block, width + SIDE)
        scale = data[:, width:].astype(F32)[:, :1]
        data = data[:, :width]
        pre_gate = lax.dot_general(data, c_gate[...], COLS, preferred_element_type=F32)
        pre_up = lax.dot_general(data, c_up[...], COLS, preferred_element_type=F32)
        project = lax.dot_general(data, c_down[...], COLS, preferred_element_type=F32)
        project = pltpu.roll(project, block - CAP, 0)
        gate_grad, up_grad, weighted, probs = swish(pre_gate, pre_up, project, scale)
        is_x = (iota(pre_gate.shape, 0) & 7) < CAP
        gate_grad = jnp.where(is_x, gate_grad, 0.0).astype(BF16)
        up_grad = jnp.where(is_x, up_grad, 0.0).astype(BF16)
        d_gate[at, :] = gate_grad
        d_up[at, :] = up_grad
        d_down[at, :] = pltpu.roll(jnp.where(is_x, weighted, 0.0), CAP, 0).astype(BF16)
        dx = jnp.dot(gate_grad, c_gate[...], preferred_element_type=F32)
        dx += jnp.dot(up_grad, c_up[...], preferred_element_type=F32)
        is_x = (iota((block, half), 0) & 7) < CAP
        ret[at, :half] = jnp.where(is_x, dx[:, :half], pltpu.roll(dx[:, half:], CAP, 0))
        probs = jnp.sum(probs, axis=1, keepdims=True)
        ret[at, half:] = jnp.broadcast_to(probs, (block, SIDE))
        for group in (2 * index, 2 * index + 1):
            away[group] = ret[rows_of(group, 1 - core), :].astype(BF16)
            side_copies[group] = start(remote(away.at[group], side.at[group], side_send.at[group], side_recv.at[group], sibling))

    def rows_of(group, which):
        return pl.ds(pl.multiple_of((group * 2 + which) * 8 * NZ, 8 * NZ), 8 * NZ)

    passes = {}

    def summed(group):
        side_copies[group].wait_recv()
        return ret[rows_of(group, core), :] + side[group].astype(F32)

    def pass_over(j):
        pass_on[j] = summed(GROUPS + j).astype(BF16)
        passes[j] = start(remote(pass_on.at[j], passed.at[j], pass_send.at[j], pass_recv.at[j], partner))

    def give_back(j):
        passes[j].wait_recv()
        value = (summed(j) + passed[j].astype(F32)).astype(BF16)
        final[j * NZ : (j + 1) * NZ] = value.reshape(NZ, 8, half + SIDE)
        ky = j % NY
        kx = lax.rem(pair + ky, 2) + 2 * (j // NY)

        def back_copy(kz):
            source = lax.rem(z + NZ - kz, NZ)
            return final.at[j * NZ + source], back_cold.at[j * NZ + z], back(kx, ky, kz)

        if j == 0:
            src, dst, to = back_copy(0)

            @pl.when(pair == 0)
            def _():
                pltpu.make_async_copy(src, dst, back_recv).start()

            @pl.when(pair == 1)
            def _():
                remote(src, dst, one_send.at[1], back_recv, to).start()

        def send_back(kz, carry):
            src, dst, to = back_copy(kz)
            remote(src, dst, back_send, back_recv, to).start()
            return carry

        lax.fori_loop(1 if j == 0 else 0, NZ, send_back, 0)

    def weight_grad(grads, out):
        data = cold[...].reshape(cold.shape[0] * 8, width + SIDE)[:, :width]
        out[...] = lax.dot_general(grads[...], data, ROWS, preferred_element_type=F32).astype(BF16)

    pairs = GROUPS // 2
    for index in range(pairs):
        compute(index)
        if index:
            give_back(2 * index - 2)
            give_back(2 * index - 1)
        compute(pairs + index)
        pass_over(2 * index)
        pass_over(2 * index + 1)
    weight_grad(d_gate, g_gate)
    give_back(GROUPS - 2)
    give_back(GROUPS - 1)
    weight_grad(d_up, g_up)
    weight_grad(d_down, g_down)

    for copy in started:
        copy.wait_send()
    for copy in mine:
        copy.wait()
    for part, send, recv in (
        (hot_x.at[others], hot_send.at[0], None),
        (hot_g.at[others], hot_send.at[1], None),
        (w.at[w_others], w_send, None),
        (cold_in.at[pl.ds(0, GROUPS * NZ - 1)], cold_send, None),
        (final.at[pl.ds(0, GROUPS * NZ - 1)], back_send, None),
        (back_w.at[pl.ds(0, RING - 1)], wb_send, wb_recv),
        (back_hot.at[pl.ds(0, NX - 1)], hb_send, hb_recv),
    ):
        remote(part, part, send, own.at[0] if recv is None else recv, sibling).wait_send()
        if recv is not None:
            remote(part, part, send, recv, sibling).wait_recv()
    remote(back_cold, back_cold, back_send, back_recv, sibling).wait_recv()

    @pl.when(pair == 1)
    def _():
        remote(cold_in.at[0], cold_in.at[0], one_send.at[0], back_recv, sibling).wait_send()
        remote(final.at[0], final.at[0], one_send.at[1], back_recv, sibling).wait_send()


def unpack_kernel(pos, cold, hot, w, own_rows, other_rows, probs, g_gate, g_up, g_down, total):
    token_count = pos.shape[1]
    half = cold.shape[1] - SIDE
    width = 2 * half
    rows = cold.shape[0]
    mine = token_count // 2
    pair, _, x, y, _ = place()
    row = iota((rows, token_count), 0)
    within = row & 7
    group = lax.div(row, 8 * NZ)
    owner_x = lax.rem(x + pair + 2 * lax.div(group, NY), NX)
    owner_y = lax.rem(y + lax.rem(group, NY), NY)
    owner = (owner_x * NY + owner_y) * NZ + lax.rem(lax.div(row, 8), NZ)
    want = owner * CAP + (within & 3)
    first = pos[0:1, :] == want
    second = pos[1:2, :] == want
    match = first | second
    pick_low = jnp.where(match & (within < CAP), 1.0, 0.0).astype(BF16)
    pick_high = jnp.where(match & (within >= CAP), 1.0, 0.0).astype(BF16)
    hot_rows = hot.shape[0]
    hot_want = CHIPS * CAP + lax.rem(iota((hot_rows, token_count), 0), HCAP)
    hot_first = pos[0:1, :] == hot_want
    hot_second = pos[1:2, :] == hot_want
    pick_hot = jnp.where(hot_first | hot_second, 1.0, 0.0).astype(BF16)
    for low, pick in ((0, pick_low), (half, pick_high)):
        part = lax.dot_general(pick, cold[:, :half], ROWS, preferred_element_type=F32)
        part += lax.dot_general(pick_hot, hot[:, low : low + half], ROWS, preferred_element_type=F32)
        total[:, low : low + half] = part
    own_rows[...] = total[pl.ds(pl.multiple_of(pair * mine, 8), mine), :]
    other_rows[...] = total[pl.ds(pl.multiple_of((1 - pair) * mine, 8), mine), :].astype(BF16)
    cold_probs = cold[:, half:].astype(F32)[:, :1]
    hot_probs = hot[:, width:].astype(F32)[:, :1]
    is_x = within < CAP
    for k, (a, b) in enumerate(((first, hot_first), (second, hot_second))):
        value = jnp.sum(jnp.where(a & is_x, cold_probs, 0.0), axis=0, keepdims=True)
        value += jnp.sum(jnp.where(b, hot_probs, 0.0), axis=0, keepdims=True)
        probs[k : k + 1, :] = value
    grads = w[0].astype(F32)
    for k in range(1, w.shape[0]):
        grads += w[k].astype(F32)
    g_gate[...] = grads[0:UNIT].astype(BF16)
    g_up[...] = grads[UNIT : 2 * UNIT].astype(BF16)
    g_down[...] = grads[2 * UNIT : 3 * UNIT].astype(BF16)


def shape(*dims, dtype=BF16):
    return jax.ShapeDtypeStruct(dims, dtype)


def local(tokens, grad_out, gate_probs, expert_ids, route_slots, hot_flags, owner_slot, cold_gate, cold_up, cold_down, hot_gate, hot_up, hot_down):
    token_count, width = tokens.shape
    wide, half = width + SIDE, width // 2
    ff = cold_gate.shape[1]
    units = 16 * RING
    dma = pltpu.SemaphoreType.DMA
    cold, hot_x, hot_g, weights, pos = pl.pallas_call(
        pack_kernel,
        out_shape=(shape(8 * CHIPS, wide), shape(HCAP, wide), shape(HCAP, width), shape(16, width), shape(2, token_count, dtype=jnp.int32)),
        in_specs=[spec(pltpu.SMEM)] * 2 + [spec(VMEM)] * 8,
        out_specs=[spec(VMEM)] * 5,
        compiler_params=params(),
    )(hot_flags, owner_slot, expert_ids.T, route_slots.T, gate_probs.T, tokens, grad_out, hot_gate, hot_up, hot_down)

    packed = half + SIDE
    lines = 8 * NZ
    hot_rows = 2 * NX * HCAP
    back_cold, back_hot, back_w, g_gate, g_up, g_down = pl.pallas_call(
        layer_kernel,
        out_shape=(shape(GROUPS * NZ, 8, packed), shape(NX, HCAP, wide), shape(RING, 16, width)) + (shape(ff, width),) * 3,
        in_specs=[spec(pl.ANY)] * 4 + [spec(VMEM)] * 3,
        out_specs=[spec(pl.ANY)] * 3 + [spec(VMEM)] * 3,
        scratch_shapes=[
            VMEM((2 * CHIPS, 8, wide), BF16), VMEM((hot_rows, wide), BF16), VMEM((hot_rows, width), BF16), VMEM((units, width), BF16),
            VMEM((16 * CHIPS, ff), BF16), VMEM((16 * CHIPS, ff), BF16), VMEM((16 * CHIPS, ff), BF16), VMEM((2 * hot_rows, units), BF16),
            VMEM((16 * CHIPS, packed), F32), VMEM((2 * GROUPS, lines, packed), BF16), VMEM((2 * GROUPS, lines, packed), BF16),
            VMEM((GROUPS, lines, packed), BF16), VMEM((GROUPS, lines, packed), BF16), VMEM((GROUPS * NZ, 8, packed), BF16),
            VMEM((hot_rows, wide), F32), VMEM((NX * HCAP, wide), BF16), VMEM((NX * HCAP, wide), BF16), VMEM((NX * HCAP, wide), BF16), VMEM((units, width), BF16),
            dma((3,)), dma, dma((GROUPS,)), dma((2,)), dma((2,)), dma, dma, dma((GROUPS,)), dma((GROUPS,)),
            dma((2 * GROUPS + 2,)), dma((2 * GROUPS + 2,)), dma((2 * GROUPS + 1,)), dma((2 * GROUPS + 1,)),
            dma((GROUPS,)), dma((GROUPS,)), dma, dma, dma, dma, dma, dma, dma((2,)),
        ],
        compiler_params=params(collective_id=0, has_side_effects=True),
    )(cold.reshape(CHIPS, 8, wide), hot_x, hot_g, weights, cold_gate[0], cold_up[0], cold_down[0])

    mine = token_count // 2
    own_rows, other_rows, probs, h_gate, h_up, h_down = pl.pallas_call(
        unpack_kernel,
        out_shape=(shape(mine, width, dtype=F32), shape(mine, width), shape(2, token_count, dtype=F32)) + (shape(UNIT, width),) * 3,
        in_specs=[spec(VMEM)] * 4,
        out_specs=[spec(VMEM)] * 6,
        scratch_shapes=[VMEM((token_count, width), F32)],
        compiler_params=params(),
    )(pos, back_cold.reshape(GROUPS * NZ * 8, packed), back_hot.reshape(NX * HCAP, wide), back_w)

    swap = [(0, 1), (1, 0)]
    pair = lax.axis_index("pair")
    halves = probs.T.reshape(2, mine, 2)
    own_probs = jnp.where(pair == 0, halves[0], halves[1])
    other_probs = jnp.where(pair == 0, halves[1], halves[0])
    summed = own_rows + lax.ppermute(other_rows, "pair", swap).astype(F32)
    summed_probs = own_probs + lax.ppermute(other_probs, "pair", swap)
    return (summed.astype(BF16), summed_probs, g_gate[None], g_up[None], g_down[None], h_gate, h_up, h_down)


def solution(mesh):
    split = P(("dp", "pair"), None)
    cold = P("dp", "pair", None)
    return jax.shard_map(
        local,
        mesh=mesh,
        in_specs=(P("dp", None),) * 5 + (P(), P()) + (cold,) * 3 + (split,) * 3,
        out_specs=(split, split, cold, cold, cold, split, split, split),
        check_vma=False,
    )
```

time: 196 us -> 131 us (0.67); the launches traced: 196 us -> 128 us
  Pallas kernels: 183 us -> 111 us
  local copies, waits for them, and re-layouts: 0 us -> 4.35 us
    pallas_call x4 -> x2, Pallas kernels: 179 us -> 108 us  [the longest x1 103 us: local(): pl.pallas_call(layer_kernel, out_shape=(shape(GROUPS * NZ, 8, packed), sh...]
    unnamed x0 -> x9, local copies, waits for them, and re-layouts: none -> 4.35 us
  transfers between devices with their start and end apart: 2 -> 2, of which waited for: 1 -> 1; matrix products, arithmetic and copies ran while one was open for 1% -> 2% of each run, Pallas kernels for 0% -> 0%
where the time goes in v2:
time: 131 us; the launch traced here: 128 us
  Pallas kernels  111 us (85%)
  waiting for transfers between devices  5.28 us (4%)
  local copies, waits for them, and re-layouts  4.35 us (3%)
  other arithmetic  4.1 us (3%)
  starting transfers between devices  2.52 us (2%)
    pallas_call x1, Pallas kernels, local(): pl.pallas_call(layer_kernel, out_shape=(shape(GROUPS * NZ, 8, packed), sh...  103 us
    ppermute x1, waiting for transfers between devices, local(): summed_probs = own_probs + lax.ppermute(other_probs, 'pair', swap)  5.28 us
    pallas_call x1, Pallas kernels, local(): pl.pallas_call(pack_kernel, out_shape=(shape(8 * CHIPS, wide), shape(HCAP...  4.8 us
    unnamed x9, local copies, waits for them, and re-layouts  4.35 us
    pallas_call x1, Pallas kernels, local(): pl.pallas_call(unpack_kernel, out_shape=(shape(mine, width, dtype=F32), s...  3.64 us
  transfers between devices with their start and end apart: 2, of which 1 were waited for; matrix products, arithmetic and copies ran while one was open for 2% of the time, Pallas kernels for 0%

profile of v2, /device:TPU:1, one launch (start us, length us, event | category | flops | bytes accessed | tf_op | source)
XLA Modules:
  0.0 128.4 jit_solution(2372943061919882006)
XLA Ops:
  0.6 4.8 %shard_map.188 = (bf16[512,1920]{1,0:T(8,128)(2,1)}, bf16[48,1920]{1,0:T(8,128)(2,1)}, bf16[48,1792]{1,0:T(8,128)(2,1)}, bf16[16,1792]{1,0:T(8,128)(2,1)}, s32[2,192]{1,0:T(2,128)}) custom-call(s32[65]{0:T(128)} %flags.1, s32[65]{0:T(128)} %owner.1, s32[2,192]{1,0:T(2,128)} %bitcast.24, s32[2,192]{1,0:T(2,128)} %bitcast.25, bf16[2,192]{1,0:T(2,128)(2,1)} %bitcast.26, ...), custom_call_target="tpu_custom_call" | custom-call | tf_op jit(solution)/shard_map/pallas_call | solution.py:464
  5.4 103.0 %shard_map.189 = (bf16[32,8,1024]{2,1,0:T(8,128)(2,1)}, bf16[4,48,1920]{2,1,0:T(8,128)(2,1)}, bf16[16,16,1792]{2,1,0:T(8,128)(2,1)}, bf16[320,1792]{1,0:T(8,128)...) custom-call(bf16[64,8,1920]{2,1,0:T(8,128)(2,1)} %bitcast.13, bf16[48,1920]{1,0:T(8,128)(2,1)} %get-tuple-element.27.hot_x_in, ...), custom_call_target="tpu_custom_call" | custom-call | tf_op jit(solution)/shard_map/pallas_call | solution.py:475
  108.5 3.6 %shard_map.190 = (f32[96,1792]{1,0:T(8,128)}, bf16[96,1792]{1,0:T(8,128)(2,1)}, f32[2,192]{1,0:T(2,128)}, bf16[5,1792]{1,0:T(8,128)(2,1)}, bf16[5,1792]{1,0:T(8,128)(2,1)}, /*index=5*/bf16[5,1792]{1,0:T(8,128)(2,1)}) custom-call(s32[2,192]{1,0:T(2,128)} %get-tuple-element.25.pos, bf16[256,1024]{1,0:T(8,128)(2,1)} %bitcast.21, bf16[192,1920]{1,0:T(8,128)(2,1)} %bitcast.20, ...), custom_call_target="tpu_custom_call" | custom-call | tf_op jit(solution)/shard_map/pallas_call | solution.py:494
  112.1 0.0 copy-start.2
  112.1 2.5 %collective-permute-start = (bf16[96,1792]{1,0:T(8,128)(2,1)}, bf16[96,1792]{1,0:T(8,128)(2,1)S(1)}, u32[]{:S(2)}, u32[]{:S(2)}) collective-permute-start(bf16[96,1792]{1,0:T(8,128)(2,1)} %get-tuple-element.34), channel_id=1, source_target_pairs={{0,1},{1,0},{2,3},{3,2},{4,5},{5,4},{6,7},{7,6},{8,9},{9,8},{10,11... | collective-permute-start | bytes 1032200 | tf_op jit(solution)/shard_map/ppermute | solution.py:508
  114.6 0.8 broadcast_select_fusion
  115.4 0.0 collective-permute-start.1
  115.5 5.3 %collective-permute-done.1 = f32[96,2]{0,1:T(2,128)S(1)} collective-permute-done((f32[96,2]{0,1:T(2,128)S(1)}, f32[96,2]{0,1:T(2,128)S(1)}, u32[]{:S(2)}, u32[]{:S(2)}) %collective-permute-start.1) | collective-permute-done | bytes 800 | tf_op jit(solution)/shard_map/ppermute | solution.py:509
  120.7 1.4 %select_add_fusion = f32[96,2]{0,1:T(2,128)} fusion(f32[96,2]{0,1:T(2,128)S(1)} %collective-permute-done.1, pred[]{:T(512)S(6)} %eq.4, f32[192,2]{0,1:T(2,128)} %bitcast.23), kind=kLoop, calls=%fused_computation.1 | loop fusion | flops 384 | bytes 3073 | tf_op jit(solution)/shard_map/add | solution.py:509
  122.1 0.0 collective-permute-done
  122.1 1.9 %add_convert_fusion = bf16[96,1792]{1,0:T(8,128)(2,1)} fusion(f32[96,1792]{1,0:T(8,128)} %get-tuple-element.33, bf16[96,1792]{1,0:T(8,128)(2,1)S(1)} %collective-permute-done), kind=kLoop, calls=%fused_computation | loop fusion | flops 516096 | bytes 1376256 | tf_op jit(solution)/shard_map/convert_element_type | solution.py:510
  124.0 0.0 copy-done.2
  124.0 0.0 copy-start.1
  124.0 1.0 copy.24
  125.0 0.7 copy-done.1
  125.7 0.0 copy-start
  125.7 1.0 copy.25
  126.7 0.7 copy-done
  127.4 1.0 copy.26
Async XLA Ops:
  112.1 11.9 %copy-start.2 = (bf16[320,1792]{1,0:T(8,128)(2,1)S(1)}, bf16[320,1792]{1,0:T(8,128)(2,1)}, u32[]{:S(2)}) copy-start(bf16[320,1792]{1,0:T(8,128)(2,1)} %get-tuple-element.36) | copy-start | bytes 3440644
  112.1 10.0 %collective-permute-start = (bf16[96,1792]{1,0:T(8,128)(2,1)}, bf16[96,1792]{1,0:T(8,128)(2,1)S(1)}, u32[]{:S(2)}, u32[]{:S(2)}) collective-permute-start(bf16[96,1792]{1,0:T(8,128)(2,1)} %get-tuple-element.34), channel_id=1, source_target_pairs={{0,1},{1,0},{2,3},{3,2},{4,5},{5,4},{6,7},{7,6},{8,9},{9,8},{10,11... | collective-permute-start | bytes 1032200 | tf_op jit(solution)/shard_map/ppermute | solution.py:508
  115.4 5.3 %collective-permute-start.1 = (f32[96,2]{0,1:T(2,128)S(1)}, f32[96,2]{0,1:T(2,128)S(1)}, u32[]{:S(2)}, u32[]{:S(2)}) collective-permute-start(f32[96,2]{0,1:T(2,128)S(1)} %broadcast_select_fusion), channel_id=1, source_target_pairs={{0,1},{1,0},{2,3},{3,2},{4,5},{5,4},{6,7},{7,6},{8,9},{9,8},{10,11... | collective-permute-start | bytes 2312 | tf_op jit(solution)/shard_map/ppermute | solution.py:509
  124.0 1.7 %copy-start.1 = (bf16[320,1792]{1,0:T(8,128)(2,1)S(1)}, bf16[320,1792]{1,0:T(8,128)(2,1)}, u32[]{:S(2)}) copy-start(bf16[320,1792]{1,0:T(8,128)(2,1)} %get-tuple-element.37) | copy-start | bytes 3440644
  125.7 1.7 %copy-start = (bf16[320,1792]{1,0:T(8,128)(2,1)S(1)}, bf16[320,1792]{1,0:T(8,128)(2,1)}, u32[]{:S(2)}) copy-start(bf16[320,1792]{1,0:T(8,128)(2,1)} %get-tuple-element.38) | copy-start | bytes 3440644

commit v3 on v2

--- a/solution.py
+++ b/solution.py
@@ -124,11 +124,11 @@
 
 def layer_kernel(
     cold_in, hot_x_in, hot_g_in, w_in, c_gate, c_up, c_down,
-    back_cold, back_hot, back_w, g_gate, g_up, g_down,
+    back_cold, back_hot, back_w, cold_out, gate_out, up_out, down_out,
     cold, hot_x, hot_g, w, d_gate, d_up, d_down, d_hot, ret, away, side, pass_on, passed, final,
-    hot_ret, hot_away, hot_side, hot_sum, w_ret,
+    hot_ret, hot_away, hot_side, hot_sum, w_ret, w_away, w_side, w_sum,
     own, cold_send, cold_recv, hot_send, hot_recv, w_send, w_recv, near_send, near_recv, over_send, over_recv,
-    side_send, side_recv, pass_send, pass_recv, back_send, back_recv, hb_send, hb_recv, wb_send, wb_recv, one_send,
+    side_send, side_recv, pass_send, pass_recv, back_send, back_recv, hb_send, hb_recv, wb_send, wb_recv, wy_send, wy_recv, one_send, out_sem,
 ):
     width = c_gate.shape[1]
     half = width // 2
@@ -169,10 +169,10 @@
 
     def send_w(k, carry):
         slot = pl.ds(pl.multiple_of(k * 16, 16), 16)
-        remote(w_in, w.at[slot], w_send, w_recv, along(0, lax.div(k, NZ), lax.rem(k, NZ))).start()
+        remote(w_in, w.at[slot], w_send, w_recv, along(0, 0, k)).start()
         return carry
 
-    lax.fori_loop(1, RING, send_w, 0)
+    lax.fori_loop(1, NZ, send_w, 0)
 
     def cold_at(group, which):
         return pl.ds((group * 2 + which) * NZ, NZ)
@@ -222,10 +222,29 @@
         start(remote(hot_g.at[this], hot_g.at[this], over_send.at[2 * GROUPS + 1], over_recv.at[2 * GROUPS + 1], sibling)),
     ]
     mine[2].wait()
-    w_others = pl.ds(0, (RING - 1) * 16)
+    w_others = pl.ds(0, (NZ - 1) * 16)
     remote(w.at[w_others], w.at[w_others], w_send, w_recv, sibling).wait_recv()
+    across = along(0, 1, 0)
+    w_here, w_there = pl.ds(0, NZ * 16), pl.ds(NZ * 16, NZ * 16)
+    w_over = start(remote(w.at[w_here], w.at[w_there], wy_send.at[0], wy_recv.at[0], across))
+
+    near, over = [], []
+
+    def hand_over(group):
+        ref = cold.at[cold_at(group, core)]
+        over.append(start(remote(ref, ref, over_send.at[group], over_recv.at[group], sibling)))
+
+    def receive(j):
+        ref = cold.at[cold_at(j, core)]
+        remote(ref, ref, cold_send, cold_recv.at[j], sibling).wait_recv()
+        to = cold.at[cold_at(GROUPS + j, core)]
+        near.append(start(remote(ref, to, near_send.at[j], near_recv.at[j], partner)))
+        hand_over(j)
+
+    receive(0)
     for copy in hot_over:
         copy.wait_recv()
+    w_over.wait_recv()
 
     units = w.shape[0]
     hot_rows = hot_x.shape[0]
@@ -249,33 +268,26 @@
     hot_swap = start(remote(hot_away, hot_side, side_send.at[2 * GROUPS], side_recv.at[2 * GROUPS], sibling))
     w_grad = lax.dot_general(d_hot[:hot_rows, :], hot_x[:, :width], ROWS, preferred_element_type=F32)
     w_grad += lax.dot_general(d_hot[hot_rows:, :], hot_g[...], ROWS, preferred_element_type=F32)
-    w_ret[...] = w_grad.astype(BF16)
+    w_ret[...] = w_grad[: NZ * 16]
+    w_away[...] = w_grad[NZ * 16 :].astype(BF16)
+    w_swap = start(remote(w_away, w_side, wy_send.at[1], wy_recv.at[1], across))
 
     def back(kx, ky, kz):
         return along(lax.rem(NX - kx, NX), ky, NZ - kz)
 
+    for j in range(1, GROUPS):
+        receive(j)
+    w_swap.wait_recv()
+    w_sum[...] = (w_ret[...] + w_side[...].astype(F32)).astype(BF16)
+
     def return_w(k, carry):
         slot = pl.ds(pl.multiple_of(k * 16, 16), 16)
-        to = back(0, lax.div(k, NZ), lax.rem(k, NZ))
-        remote(w_ret.at[slot], back_w.at[k], wb_send, wb_recv, to).start()
+        remote(w_sum.at[slot], back_w.at[k], wb_send, wb_recv, back(0, 0, k)).start()
         return carry
 
-    lax.fori_loop(1, RING, return_w, 0)
-    mine = [pltpu.make_async_copy(w_ret.at[pl.ds(0, 16)], back_w.at[0], own.at[0])]
+    lax.fori_loop(1, NZ, return_w, 0)
+    mine = [pltpu.make_async_copy(w_sum.at[pl.ds(0, 16)], back_w.at[0], own.at[0])]
     mine[0].start()
-
-    near, over = [], []
-
-    def hand_over(group):
-        ref = cold.at[cold_at(group, core)]
-        over.append(start(remote(ref, ref, over_send.at[group], over_recv.at[group], sibling)))
-
-    for j in range(GROUPS):
-        ref = cold.at[cold_at(j, core)]
-        remote(ref, ref, cold_send, cold_recv.at[j], sibling).wait_recv()
-        to = cold.at[cold_at(GROUPS + j, core)]
-        near.append(start(remote(ref, to, near_send.at[j], near_recv.at[j], partner)))
-        hand_over(j)
     hot_swap.wait_recv()
     for k in range(NX):
         at = pl.ds(k * HCAP, HCAP)
@@ -363,10 +375,6 @@
 
         lax.fori_loop(1 if j == 0 else 0, NZ, send_back, 0)
 
-    def weight_grad(grads, out):
-        data = cold[...].reshape(cold.shape[0] * 8, width + SIDE)[:, :width]
-        out[...] = lax.dot_general(grads[...], data, ROWS, preferred_element_type=F32).astype(BF16)
-
     pairs = GROUPS // 2
     for index in range(pairs):
         compute(index)
@@ -376,11 +384,11 @@
         compute(pairs + index)
         pass_over(2 * index)
         pass_over(2 * index + 1)
-    weight_grad(d_gate, g_gate)
+    for k, (source, out) in enumerate(((cold, cold_out), (d_gate, gate_out), (d_up, up_out), (d_down, down_out))):
+        mine.append(pltpu.make_async_copy(source, out, out_sem.at[k]))
+        mine[-1].start()
     give_back(GROUPS - 2)
     give_back(GROUPS - 1)
-    weight_grad(d_up, g_up)
-    weight_grad(d_down, g_down)
 
     for copy in started:
         copy.wait_send()
@@ -392,7 +400,7 @@
         (w.at[w_others], w_send, None),
         (cold_in.at[pl.ds(0, GROUPS * NZ - 1)], cold_send, None),
         (final.at[pl.ds(0, GROUPS * NZ - 1)], back_send, None),
-        (back_w.at[pl.ds(0, RING - 1)], wb_send, wb_recv),
+        (back_w.at[pl.ds(0, NZ - 1)], wb_send, wb_recv),
         (back_hot.at[pl.ds(0, NX - 1)], hb_send, hb_recv),
     ):
         remote(part, part, send, own.at[0] if recv is None else recv, sibling).wait_send()
@@ -406,7 +414,7 @@
         remote(final.at[0], final.at[0], one_send.at[1], back_recv, sibling).wait_send()
 
 
-def unpack_kernel(pos, cold, hot, w, own_rows, other_rows, probs, g_gate, g_up, g_down, total):
+def unpack_kernel(pos, cold, hot, w, own_rows, other_rows, g_gate, g_up, g_down, total):
     token_count = pos.shape[1]
     half = cold.shape[1] - SIDE
     width = 2 * half
@@ -423,32 +431,41 @@
     first = pos[0:1, :] == want
     second = pos[1:2, :] == want
     match = first | second
-    pick_low = jnp.where(match & (within < CAP), 1.0, 0.0).astype(BF16)
-    pick_high = jnp.where(match & (within >= CAP), 1.0, 0.0).astype(BF16)
+
+    def pick(mask):
+        return jnp.where(mask, 1.0, 0.0).astype(BF16)
+
+    pick_low = pick(match & (within < CAP))
+    pick_high = pick(match & (within >= CAP))
     hot_rows = hot.shape[0]
     hot_want = CHIPS * CAP + lax.rem(iota((hot_rows, token_count), 0), HCAP)
     hot_first = pos[0:1, :] == hot_want
     hot_second = pos[1:2, :] == hot_want
-    pick_hot = jnp.where(hot_first | hot_second, 1.0, 0.0).astype(BF16)
-    for low, pick in ((0, pick_low), (half, pick_high)):
-        part = lax.dot_general(pick, cold[:, :half], ROWS, preferred_element_type=F32)
+    pick_hot = pick(hot_first | hot_second)
+    for low, cold_pick in ((0, pick_low), (half, pick_high)):
+        part = lax.dot_general(cold_pick, cold[:, :half], ROWS, preferred_element_type=F32)
         part += lax.dot_general(pick_hot, hot[:, low : low + half], ROWS, preferred_element_type=F32)
         total[:, low : low + half] = part
+    is_x = within < CAP
+    values = []
+    for a, b in ((first, hot_first), (second, hot_second)):
+        value = lax.dot_general(pick(a & is_x), cold[:, half:], ROWS, preferred_element_type=F32)
+        values.append(value + lax.dot_general(pick(b), hot[:, width:], ROWS, preferred_element_type=F32))
+    total[:, width:] = jnp.where(iota((token_count, SIDE), 1) == 0, values[0], values[1])
     own_rows[...] = total[pl.ds(pl.multiple_of(pair * mine, 8), mine), :]
     other_rows[...] = total[pl.ds(pl.multiple_of((1 - pair) * mine, 8), mine), :].astype(BF16)
-    cold_probs = cold[:, half:].astype(F32)[:, :1]
-    hot_probs = hot[:, width:].astype(F32)[:, :1]
-    is_x = within < CAP
-    for k, (a, b) in enumerate(((first, hot_first), (second, hot_second))):
-        value = jnp.sum(jnp.where(a & is_x, cold_probs, 0.0), axis=0, keepdims=True)
-        value += jnp.sum(jnp.where(b, hot_probs, 0.0), axis=0, keepdims=True)
-        probs[k : k + 1, :] = value
     grads = w[0].astype(F32)
     for k in range(1, w.shape[0]):
         grads += w[k].astype(F32)
     g_gate[...] = grads[0:UNIT].astype(BF16)
     g_up[...] = grads[UNIT : 2 * UNIT].astype(BF16)
     g_down[...] = grads[2 * UNIT : 3 * UNIT].astype(BF16)
+
+
+def weight_kernel(cold, d_gate, d_up, d_down, g_gate, g_up, g_down):
+    width = g_gate.shape[1]
+    for grads, out in ((d_gate, g_gate), (d_up, g_up), (d_down, g_down)):
+        out[...] = lax.dot_general(grads[...], cold[:, :width], ROWS, preferred_element_type=F32).astype(BF16)
 
 
 def shape(*dims, dtype=BF16):
@@ -472,42 +489,46 @@
     packed = half + SIDE
     lines = 8 * NZ
     hot_rows = 2 * NX * HCAP
-    back_cold, back_hot, back_w, g_gate, g_up, g_down = pl.pallas_call(
+    back_cold, back_hot, back_w, rows, d_gate, d_up, d_down = pl.pallas_call(
         layer_kernel,
-        out_shape=(shape(GROUPS * NZ, 8, packed), shape(NX, HCAP, wide), shape(RING, 16, width)) + (shape(ff, width),) * 3,
+        out_shape=(shape(GROUPS * NZ, 8, packed), shape(NX, HCAP, wide), shape(NZ, 16, width), shape(2 * CHIPS, 8, wide)) + (shape(16 * CHIPS, ff),) * 3,
         in_specs=[spec(pl.ANY)] * 4 + [spec(VMEM)] * 3,
-        out_specs=[spec(pl.ANY)] * 3 + [spec(VMEM)] * 3,
+        out_specs=[spec(pl.ANY)] * 7,
         scratch_shapes=[
             VMEM((2 * CHIPS, 8, wide), BF16), VMEM((hot_rows, wide), BF16), VMEM((hot_rows, width), BF16), VMEM((units, width), BF16),
             VMEM((16 * CHIPS, ff), BF16), VMEM((16 * CHIPS, ff), BF16), VMEM((16 * CHIPS, ff), BF16), VMEM((2 * hot_rows, units), BF16),
             VMEM((16 * CHIPS, packed), F32), VMEM((2 * GROUPS, lines, packed), BF16), VMEM((2 * GROUPS, lines, packed), BF16),
             VMEM((GROUPS, lines, packed), BF16), VMEM((GROUPS, lines, packed), BF16), VMEM((GROUPS * NZ, 8, packed), BF16),
-            VMEM((hot_rows, wide), F32), VMEM((NX * HCAP, wide), BF16), VMEM((NX * HCAP, wide), BF16), VMEM((NX * HCAP, wide), BF16), VMEM((units, width), BF16),
+            VMEM((hot_rows, wide), F32), VMEM((NX * HCAP, wide), BF16), VMEM((NX * HCAP, wide), BF16), VMEM((NX * HCAP, wide), BF16), VMEM((NZ * 16, width), F32), VMEM((NZ * 16, width), BF16), VMEM((NZ * 16, width), BF16), VMEM((NZ * 16, width), BF16),
             dma((3,)), dma, dma((GROUPS,)), dma((2,)), dma((2,)), dma, dma, dma((GROUPS,)), dma((GROUPS,)),
             dma((2 * GROUPS + 2,)), dma((2 * GROUPS + 2,)), dma((2 * GROUPS + 1,)), dma((2 * GROUPS + 1,)),
-            dma((GROUPS,)), dma((GROUPS,)), dma, dma, dma, dma, dma, dma, dma((2,)),
+            dma((GROUPS,)), dma((GROUPS,)), dma, dma, dma, dma, dma, dma, dma((2,)), dma((2,)), dma((2,)), dma((4,)),
         ],
         compiler_params=params(collective_id=0, has_side_effects=True),
     )(cold.reshape(CHIPS, 8, wide), hot_x, hot_g, weights, cold_gate[0], cold_up[0], cold_down[0])
 
     mine = token_count // 2
-    own_rows, other_rows, probs, h_gate, h_up, h_down = pl.pallas_call(
+    own_rows, other_rows, h_gate, h_up, h_down = pl.pallas_call(
         unpack_kernel,
-        out_shape=(shape(mine, width, dtype=F32), shape(mine, width), shape(2, token_count, dtype=F32)) + (shape(UNIT, width),) * 3,
+        out_shape=(shape(mine, wide, dtype=F32), shape(mine, wide)) + (shape(UNIT, width),) * 3,
         in_specs=[spec(VMEM)] * 4,
-        out_specs=[spec(VMEM)] * 6,
-        scratch_shapes=[VMEM((token_count, width), F32)],
+        out_specs=[spec(VMEM)] * 5,
+        scratch_shapes=[VMEM((token_count, wide), F32)],
         compiler_params=params(),
     )(pos, back_cold.reshape(GROUPS * NZ * 8, packed), back_hot.reshape(NX * HCAP, wide), back_w)
 
-    swap = [(0, 1), (1, 0)]
-    pair = lax.axis_index("pair")
-    halves = probs.T.reshape(2, mine, 2)
-    own_probs = jnp.where(pair == 0, halves[0], halves[1])
-    other_probs = jnp.where(pair == 0, halves[1], halves[0])
-    summed = own_rows + lax.ppermute(other_rows, "pair", swap).astype(F32)
-    summed_probs = own_probs + lax.ppermute(other_probs, "pair", swap)
-    return (summed.astype(BF16), summed_probs, g_gate[None], g_up[None], g_down[None], h_gate, h_up, h_down)
+    swapped = lax.ppermute(other_rows, "pair", [(0, 1), (1, 0)])
+    count = 16 * CHIPS
+    g_gate, g_up, g_down = pl.pallas_call(
+        weight_kernel,
+        out_shape=(shape(ff, width),) * 3,
+        in_specs=[spec(VMEM)] * 4,
+        out_specs=[spec(VMEM)] * 3,
+        cost_estimate=pl.CostEstimate(flops=6 * count * ff * width, bytes_accessed=2 * count * (wide + 3 * ff) + 6 * ff * width, transcendentals=0),
+        compiler_params=params(),
+    )(rows.reshape(count, wide), d_gate, d_up, d_down)
+    summed = own_rows + swapped.astype(F32)
+    return (summed[:, :width].astype(BF16), summed[:, width : width + 2], g_gate[None], g_up[None], g_down[None], h_gate, h_up, h_down)
 
 
 def solution(mesh):

time: 131 us -> 128 us (0.977); the launches traced: 128 us -> 127 us
  Pallas kernels: 111 us -> 124 us
  waiting for transfers between devices: 5.28 us -> 0.47 us
  other arithmetic: 4.1 us -> 0.06 us
  local copies, waits for them, and re-layouts: 4.35 us -> 1.41 us
  starting transfers between devices: 2.52 us -> 0.01 us
    pallas_call x1 -> x2, Pallas kernels: 3.64 us -> 11.3 us  [the longest x1 7.66 us: local(): pl.pallas_call(weight_kernel, out_shape=(shape(ff, width),) * 3, in_specs...]
    pallas_call x1, Pallas kernels: 103 us -> 108 us  [local(): pl.pallas_call(layer_kernel, out_shape=(shape(GROUPS * NZ, 8, packed), sh...]
    ppermute x2 -> x1, waiting for transfers between devices: 5.28 us -> 0.47 us  [local(): swapped = lax.ppermute(other_rows, 'pair', [(0, 1), (1, 0)])]
    unnamed x9 -> x3, local copies, waits for them, and re-layouts: 4.35 us -> 0.64 us
    ppermute x2 -> x1, starting transfers between devices: 2.52 us -> 0.01 us  [local(): swapped = lax.ppermute(other_rows, 'pair', [(0, 1), (1, 0)])]
    convert_element_type x1 -> x0, other arithmetic: 1.89 us -> none  [local(): summed.astype(BF16)]
    add x1, other arithmetic: 1.39 us -> 0.06 us  [local(): summed = own_rows + swapped.astype(F32)]
  transfers between devices with their start and end apart: 2 -> 1, of which waited for: 1 -> 1; matrix products, arithmetic and copies ran while one was open for 2% -> 0% of each run, Pallas kernels for 0% -> 6%
where the time goes in v3:
time: 128 us; the launch traced here: 127 us
  Pallas kernels  124 us (97%)
  local copies, waits for them, and re-layouts  1.41 us (1%)
    pallas_call x1, Pallas kernels, local(): pl.pallas_call(layer_kernel, out_shape=(shape(GROUPS * NZ, 8, packed), sh...  108 us
    pallas_call x1, Pallas kernels, local(): pl.pallas_call(weight_kernel, out_shape=(shape(ff, width),) * 3, in_specs...  7.66 us
    pallas_call x1, Pallas kernels, local(): pl.pallas_call(pack_kernel, out_shape=(shape(8 * CHIPS, wide), shape(HCAP...  4.8 us
    pallas_call x1, Pallas kernels, local(): pl.pallas_call(unpack_kernel, out_shape=(shape(mine, wide, dtype=F32), sh...  3.59 us
  transfers between devices with their start and end apart: 1, of which 1 were waited for; matrix products, arithmetic and copies ran while one was open for 0% of the time, Pallas kernels for 6%

profile of v3, /device:TPU:1, one launch (start us, length us, event | category | flops | bytes accessed | tf_op | source)
XLA Modules:
  0.0 126.9 jit_solution(14102047166588375942)
XLA Ops:
  0.6 4.8 %shard_map.188 = (bf16[512,1920]{1,0:T(8,128)(2,1)}, bf16[48,1920]{1,0:T(8,128)(2,1)}, bf16[48,1792]{1,0:T(8,128)(2,1)}, bf16[16,1792]{1,0:T(8,128)(2,1)}, s32[2,192]{1,0:T(2,128)}) custom-call(s32[65]{0:T(128)} %flags.1, s32[65]{0:T(128)} %owner.1, s32[2,192]{1,0:T(2,128)} %bitcast.19, s32[2,192]{1,0:T(2,128)} %bitcast.20, bf16[2,192]{1,0:T(2,128)(2,1)} %bitcast.21, ...), custom_call_target="tpu_custom_call" | custom-call | tf_op jit(solution)/shard_map/pallas_call | solution.py:481
  5.4 108.2 %shard_map.189 = (bf16[32,8,1024]{2,1,0:T(8,128)(2,1)}, bf16[4,48,1920]{2,1,0:T(8,128)(2,1)}, bf16[8,16,1792]{2,1,0:T(8,128)(2,1)}, bf16[128,8,1920]{2,1,0:T(8,1...) custom-call(bf16[64,8,1920]{2,1,0:T(8,128)(2,1)} %bitcast.13, ...), custom_call_target="tpu_custom_call" | custom-call | tf_op jit(solution)/shard_map/pallas_call | solution.py:492
  113.6 3.6 %shard_map.190 = (f32[96,1920]{1,0:T(8,128)}, bf16[96,1920]{1,0:T(8,128)(2,1)}, bf16[5,1792]{1,0:T(8,128)(2,1)}, bf16[5,1792]{1,0:T(8,128)(2,1)}, bf16[5,1792]{1,0:T(8,128)(2,1)}) custom-call(s32[2,192]{1,0:T(2,128)} %get-tuple-element.28.pos, bf16[256,1024]{1,0:T(8,128)(2,1)} %bitcast.18, bf16[192,1920]{1,0:T(8,128)(2,1)} %bitcast.17, ...), custom_call_target="tpu_custom_call" | custom-call | tf_op jit(solution)/shard_map/pallas_call | solution.py:511
  117.2 0.0 collective-permute-start
  117.2 0.0 copy-start
  117.2 7.7 %shard_map.191 = (bf16[320,1792]{1,0:T(8,128)(2,1)}, bf16[320,1792]{1,0:T(8,128)(2,1)}, bf16[320,1792]{1,0:T(8,128)(2,1)}) custom-call(bf16[1024,1920]{1,0:T(8,128)(2,1)} %bitcast.22, bf16[1024,320]{1,0:T(8,128)(2,1)} %get-tuple-element.39.d_gate, bf16[1024,320]{1,0:T(8,128)(2,1)} %get-tuple-element.40.d_up, bf16[1024,320]{1,0:T(8,128)(2,1)} %get-tuple-element.41.d_down), custom_call_target="tpu_custom_call" | custom-call | flops 3523215360 | bytes 9338880 | tf_op jit(solution)/shard_map/pallas_call | solution.py:522
  124.9 0.5 collective-permute-done
  125.4 0.0 copy-done
  125.4 0.1 convert_add_fusion
  125.5 0.8 slice.12
  126.2 0.6 copy.21
  (1 shorter events, 0.0 us)
Async XLA Ops:
  117.2 8.1 %collective-permute-start = (bf16[96,1920]{1,0:T(8,128)(2,1)}, bf16[96,1920]{1,0:T(8,128)(2,1)S(1)}, u32[]{:S(2)}, u32[]{:S(2)}) collective-permute-start(bf16[96,1920]{1,0:T(8,128)(2,1)} %get-tuple-element.37), channel_id=1, source_target_pairs={{0,1},{1,0},{2,3},{3,2},{4,5},{5,4},{6,7},{7,6},{8,9},{9,8},{10,11... | collective-permute-start | bytes 1105928 | tf_op jit(solution)/shard_map/ppermute | solution.py:520
  117.2 8.1 %copy-start = (f32[96,1920]{1,0:T(8,128)S(1)}, f32[96,1920]{1,0:T(8,128)}, u32[]{:S(2)}) copy-start(f32[96,1920]{1,0:T(8,128)} %get-tuple-element.36) | copy-start | bytes 2211844

commit v4 on v3

--- a/solution.py
+++ b/solution.py
@@ -52,48 +52,6 @@
     out[...] = jnp.where(hot == 1, hot_row, cold_row)
 
 
-def cold_match(pos, low, rows, token_count):
-    row = low + iota((rows, token_count), 0)
-    within = row & 7
-    return row, within, (row >> 3) * CAP + (within & 3)
-
-
-def pack_kernel(flags, owner, ids, slots, probs, tokens, grad, gate, up, down, cold, hot_x, hot_g, weights, pos):
-    positions_kernel(flags, owner, ids, slots, pos)
-    token_count, width = tokens.shape
-    block = 8 * min(CHIPS, 16)
-    gates = probs[...].astype(F32)
-
-    def step(index, carry):
-        low = pl.multiple_of(index * block, block)
-        row, within, want = cold_match(pos, low, block, token_count)
-        first = pos[0:1, :] == want
-        second = pos[1:2, :] == want
-        match = first | second
-        pick_x = jnp.where(match & (within < CAP), 1.0, 0.0).astype(BF16)
-        pick_g = jnp.where(match & (within >= CAP), 1.0, 0.0).astype(BF16)
-        rows = jnp.dot(pick_x, tokens[...], preferred_element_type=F32)
-        rows += jnp.dot(pick_g, grad[...], preferred_element_type=F32)
-        cold[pl.ds(low, block), :width] = rows.astype(BF16)
-        scale = jnp.where(first, gates[0:1, :], 0.0) + jnp.where(second, gates[1:2, :], 0.0)
-        scale = jnp.sum(scale, axis=1, keepdims=True)
-        cold[pl.ds(low, block), width:] = jnp.broadcast_to(scale, (block, SIDE)).astype(BF16)
-        return carry
-
-    lax.fori_loop(0, 8 * CHIPS // block, step, 0)
-    want = CHIPS * CAP + iota((HCAP, token_count), 0)
-    first = pos[0:1, :] == want
-    second = pos[1:2, :] == want
-    pick = jnp.where(first | second, 1.0, 0.0).astype(BF16)
-    hot_x[:, :width] = jnp.dot(pick, tokens[...], preferred_element_type=F32).astype(BF16)
-    hot_g[...] = jnp.dot(pick, grad[...], preferred_element_type=F32).astype(BF16)
-    scale = jnp.where(first, gates[0:1, :], 0.0) + jnp.where(second, gates[1:2, :], 0.0)
-    hot_x[:, width:] = jnp.broadcast_to(jnp.sum(scale, axis=1, keepdims=True), (HCAP, SIDE)).astype(BF16)
-    rest = jnp.zeros((16 - 3 * UNIT, width), F32)
-    parts = [gate[...].astype(F32), up[...].astype(F32), down[...].astype(F32), rest]
-    weights[...] = jnp.concatenate(parts, axis=0).astype(BF16)
-
-
 def place():
     me = lax.axis_index("dp")
     core = lax.rem(me, 2)
@@ -122,17 +80,25 @@
     return gate_grad, hidden_grad * act, scale * hidden, probs
 
 
+def one_hot(mask):
+    return jnp.where(mask, 1.0, 0.0).astype(BF16)
+
+
 def layer_kernel(
-    cold_in, hot_x_in, hot_g_in, w_in, c_gate, c_up, c_down,
-    back_cold, back_hot, back_w, cold_out, gate_out, up_out, down_out,
-    cold, hot_x, hot_g, w, d_gate, d_up, d_down, d_hot, ret, away, side, pass_on, passed, final,
+    flags, owner, ids, slots, probs_in, tokens, grad, gate, up, down, c_gate_in, c_up_in, c_down_in,
+    pos, back_cold, back_hot, back_w, cold_out, gate_out, up_out, down_out,
+    c_gate, c_up, c_down, cold_in, hot_x_in, hot_g_in, w_in, cold, hot_x, hot_g, w, d_gate, d_up, d_down, d_hot, ret, away, side, pass_on, passed, final,
     hot_ret, hot_away, hot_side, hot_sum, w_ret, w_away, w_side, w_sum,
     own, cold_send, cold_recv, hot_send, hot_recv, w_send, w_recv, near_send, near_recv, over_send, over_recv,
-    side_send, side_recv, pass_send, pass_recv, back_send, back_recv, hb_send, hb_recv, wb_send, wb_recv, wy_send, wy_recv, one_send, out_sem,
+    side_send, side_recv, pass_send, pass_recv, back_send, back_recv, hb_send, hb_recv, wb_send, wb_recv, wy_send, wy_recv, one_send, out_sem, load_sem,
 ):
-    width = c_gate.shape[1]
+    token_count, width = tokens.shape
     half = width // 2
     pair, core, x, y, z = place()
+    loads = []
+    for k, (source, to) in enumerate(((c_gate_in, c_gate), (c_up_in, c_up), (c_down_in, c_down))):
+        loads.append(pltpu.make_async_copy(source, to, load_sem.at[k]))
+        loads[k].start()
     sibling = device(x, y, z, 1 - core, pair)
     partner = device(x, y, z, core, 1 - pair)
 
@@ -151,6 +117,39 @@
     lax.fori_loop(1, CHIPS, greet, 0)
     pl.semaphore_signal(barrier, inc=1, device_id=sibling, device_id_type=MESH)
     pl.semaphore_signal(barrier, inc=1, device_id=partner, device_id_type=MESH)
+
+    positions_kernel(flags, owner, ids, slots, pos)
+    gates = probs_in[...].astype(F32)
+
+    def scale_of(first, second):
+        scale = jnp.where(first, gates[0:1, :], 0.0) + jnp.where(second, gates[1:2, :], 0.0)
+        return jnp.broadcast_to(jnp.sum(scale, axis=1, keepdims=True), (first.shape[0], SIDE)).astype(BF16)
+
+    want = CHIPS * CAP + iota((HCAP, token_count), 0)
+    first, second = pos[0:1, :] == want, pos[1:2, :] == want
+    pick = one_hot(first | second)
+    hot_x_in[:, :width] = jnp.dot(pick, tokens[...], preferred_element_type=F32).astype(BF16)
+    hot_g_in[...] = jnp.dot(pick, grad[...], preferred_element_type=F32).astype(BF16)
+    hot_x_in[:, width:] = scale_of(first, second)
+    rest = jnp.zeros((16 - 3 * UNIT, width), F32)
+    parts = [gate[...].astype(F32), up[...].astype(F32), down[...].astype(F32), rest]
+    w_in[...] = jnp.concatenate(parts, axis=0).astype(BF16)
+
+    def pack(j):
+        base = (lax.rem(x + pair + 2 * (j // NY), NX) * NY + lax.rem(y + j % NY, NY)) * NZ
+        row = iota((8 * NZ, token_count), 0)
+        within = row & 7
+        want = (base + (row >> 3)) * CAP + (within & 3)
+        first, second = pos[0:1, :] == want, pos[1:2, :] == want
+        match = first | second
+        rows = jnp.dot(one_hot(match & (within < CAP)), tokens[...], preferred_element_type=F32)
+        rows += jnp.dot(one_hot(match & (within >= CAP)), grad[...], preferred_element_type=F32)
+        at = slice(j * NZ, (j + 1) * NZ)
+        cold_in[at, :, :width] = rows.astype(BF16).reshape(NZ, 8, width)
+        cold_in[at, :, width:] = scale_of(first, second).reshape(NZ, 8, SIDE)
+
+    for j in range(GROUPS):
+        pack(j)
     pl.semaphore_wait(barrier, CHIPS + 1)
 
     def hot_at(which, k):
@@ -177,14 +176,12 @@
     def cold_at(group, which):
         return pl.ds((group * 2 + which) * NZ, NZ)
 
-    for j in range(GROUPS):
+    def issue(j):
         kx, ky = pair + 2 * (j // NY), j % NY
-        to_x, to_y = lax.rem(x + kx, NX), lax.rem(y + ky, NY)
-
-        def cold_copy(kz, j=j, kx=kx, ky=ky, to_x=to_x, to_y=to_y):
-            chip = (to_x * NY + to_y) * NZ + lax.rem(z + kz, NZ)
+
+        def cold_copy(kz):
             slot = (j * 2 + core) * NZ + z
-            return cold_in.at[chip], cold.at[slot], along(kx, ky, kz)
+            return cold_in.at[j * NZ + lax.rem(z + kz, NZ)], cold.at[slot], along(kx, ky, kz)
 
         if j == 0:
             src, dst, to = cold_copy(0)
@@ -197,12 +194,15 @@
             def _():
                 remote(src, dst, one_send.at[0], cold_recv.at[0], to).start()
 
-        def send_cold(kz, carry, j=j, cold_copy=cold_copy):
+        def send_cold(kz, carry):
             src, dst, to = cold_copy(kz)
             remote(src, dst, cold_send, cold_recv.at[j], to).start()
             return carry
 
         lax.fori_loop(1 if j == 0 else 0, NZ, send_cold, 0)
+
+    issue(0)
+    issue(1)
 
     started = []
 
@@ -228,11 +228,11 @@
     w_here, w_there = pl.ds(0, NZ * 16), pl.ds(NZ * 16, NZ * 16)
     w_over = start(remote(w.at[w_here], w.at[w_there], wy_send.at[0], wy_recv.at[0], across))
 
-    near, over = [], []
+    near, over = [], {}
 
     def hand_over(group):
         ref = cold.at[cold_at(group, core)]
-        over.append(start(remote(ref, ref, over_send.at[group], over_recv.at[group], sibling)))
+        over[group] = start(remote(ref, ref, over_send.at[group], over_recv.at[group], sibling))
 
     def receive(j):
         ref = cold.at[cold_at(j, core)]
@@ -240,8 +240,11 @@
         to = cold.at[cold_at(GROUPS + j, core)]
         near.append(start(remote(ref, to, near_send.at[j], near_recv.at[j], partner)))
         hand_over(j)
+        if j + 2 < GROUPS:
+            issue(j + 2)
 
     receive(0)
+    receive(1)
     for copy in hot_over:
         copy.wait_recv()
     w_over.wait_recv()
@@ -275,30 +278,33 @@
     def back(kx, ky, kz):
         return along(lax.rem(NX - kx, NX), ky, NZ - kz)
 
-    for j in range(1, GROUPS):
-        receive(j)
-    w_swap.wait_recv()
-    w_sum[...] = (w_ret[...] + w_side[...].astype(F32)).astype(BF16)
-
-    def return_w(k, carry):
-        slot = pl.ds(pl.multiple_of(k * 16, 16), 16)
-        remote(w_sum.at[slot], back_w.at[k], wb_send, wb_recv, back(0, 0, k)).start()
-        return carry
-
-    lax.fori_loop(1, NZ, return_w, 0)
-    mine = [pltpu.make_async_copy(w_sum.at[pl.ds(0, 16)], back_w.at[0], own.at[0])]
-    mine[0].start()
-    hot_swap.wait_recv()
-    for k in range(NX):
-        at = pl.ds(k * HCAP, HCAP)
-        source = pl.ds(pl.multiple_of((core * NX + k) * HCAP, HCAP), HCAP)
-        hot_sum[at, :] = (hot_ret[source, :] + hot_side[at, :].astype(F32)).astype(BF16)
-        if k:
-            remote(hot_sum.at[at], back_hot.at[k], hb_send, hb_recv, back(k, 0, 0)).start()
-        else:
-            mine.append(pltpu.make_async_copy(hot_sum.at[at], back_hot.at[0], own.at[1]))
-            mine[1].start()
-    for j in range(GROUPS):
+    mine = []
+
+    def return_weights():
+        w_swap.wait_recv()
+        w_sum[...] = (w_ret[...] + w_side[...].astype(F32)).astype(BF16)
+
+        def return_w(k, carry):
+            slot = pl.ds(pl.multiple_of(k * 16, 16), 16)
+            remote(w_sum.at[slot], back_w.at[k], wb_send, wb_recv, back(0, 0, k)).start()
+            return carry
+
+        lax.fori_loop(1, NZ, return_w, 0)
+        mine.append(pltpu.make_async_copy(w_sum.at[pl.ds(0, 16)], back_w.at[0], own.at[0]))
+        mine[-1].start()
+    def return_hot():
+        hot_swap.wait_recv()
+        for k in range(NX):
+            at = pl.ds(k * HCAP, HCAP)
+            source = pl.ds(pl.multiple_of((core * NX + k) * HCAP, HCAP), HCAP)
+            hot_sum[at, :] = (hot_ret[source, :] + hot_side[at, :].astype(F32)).astype(BF16)
+            if k:
+                remote(hot_sum.at[at], back_hot.at[k], hb_send, hb_recv, back(k, 0, 0)).start()
+            else:
+                mine.append(pltpu.make_async_copy(hot_sum.at[at], back_hot.at[0], own.at[1]))
+                mine[-1].start()
+
+    def relay(j):
         near[j].wait_recv()
         hand_over(GROUPS + j)
 
@@ -375,18 +381,40 @@
 
         lax.fori_loop(1 if j == 0 else 0, NZ, send_back, 0)
 
-    pairs = GROUPS // 2
-    for index in range(pairs):
-        compute(index)
-        if index:
-            give_back(2 * index - 2)
-            give_back(2 * index - 1)
-        compute(pairs + index)
-        pass_over(2 * index)
-        pass_over(2 * index + 1)
-    for k, (source, out) in enumerate(((cold, cold_out), (d_gate, gate_out), (d_up, up_out), (d_down, down_out))):
+    def keep(k, source, out):
         mine.append(pltpu.make_async_copy(source, out, out_sem.at[k]))
         mine[-1].start()
+
+    for copy in loads:
+        copy.wait()
+    relay(0)
+    relay(1)
+    for j in range(2, GROUPS):
+        if j == 2:
+            receive(2)
+        if j == 3:
+            compute(0)
+            receive(3)
+    if GROUPS == 2:
+        compute(0)
+    compute(GROUPS // 2)
+    return_weights()
+    return_hot()
+    pass_over(0)
+    pass_over(1)
+    if GROUPS > 2:
+        relay(2)
+        compute(1)
+        relay(3)
+        give_back(0)
+        give_back(1)
+        compute(3)
+        pass_over(2)
+        pass_over(3)
+    keep(0, cold, cold_out)
+    keep(1, d_gate, gate_out)
+    keep(2, d_up, up_out)
+    keep(3, d_down, down_out)
     give_back(GROUPS - 2)
     give_back(GROUPS - 1)
 
@@ -431,17 +459,13 @@
     first = pos[0:1, :] == want
     second = pos[1:2, :] == want
     match = first | second
-
-    def pick(mask):
-        return jnp.where(mask, 1.0, 0.0).astype(BF16)
-
-    pick_low = pick(match & (within < CAP))
-    pick_high = pick(match & (within >= CAP))
+    pick_low = one_hot(match & (within < CAP))
+    pick_high = one_hot(match & (within >= CAP))
     hot_rows = hot.shape[0]
     hot_want = CHIPS * CAP + lax.rem(iota((hot_rows, token_count), 0), HCAP)
     hot_first = pos[0:1, :] == hot_want
     hot_second = pos[1:2, :] == hot_want
-    pick_hot = pick(hot_first | hot_second)
+    pick_hot = one_hot(hot_first | hot_second)
     for low, cold_pick in ((0, pick_low), (half, pick_high)):
         part = lax.dot_general(cold_pick, cold[:, :half], ROWS, preferred_element_type=F32)
         part += lax.dot_general(pick_hot, hot[:, low : low + half], ROWS, preferred_element_type=F32)
@@ -449,8 +473,8 @@
     is_x = within < CAP
     values = []
     for a, b in ((first, hot_first), (second, hot_second)):
-        value = lax.dot_general(pick(a & is_x), cold[:, half:], ROWS, preferred_element_type=F32)
-        values.append(value + lax.dot_general(pick(b), hot[:, width:], ROWS, preferred_element_type=F32))
+        value = lax.dot_general(one_hot(a & is_x), cold[:, half:], ROWS, preferred_element_type=F32)
+        values.append(value + lax.dot_general(one_hot(b), hot[:, width:], ROWS, preferred_element_type=F32))
     total[:, width:] = jnp.where(iota((token_count, SIDE), 1) == 0, values[0], values[1])
     own_rows[...] = total[pl.ds(pl.multiple_of(pair * mine, 8), mine), :]
     other_rows[...] = total[pl.ds(pl.multiple_of((1 - pair) * mine, 8), mine), :].astype(BF16)
@@ -478,23 +502,17 @@
     ff = cold_gate.shape[1]
     units = 16 * RING
     dma = pltpu.SemaphoreType.DMA
-    cold, hot_x, hot_g, weights, pos = pl.pallas_call(
-        pack_kernel,
-        out_shape=(shape(8 * CHIPS, wide), shape(HCAP, wide), shape(HCAP, width), shape(16, width), shape(2, token_count, dtype=jnp.int32)),
-        in_specs=[spec(pltpu.SMEM)] * 2 + [spec(VMEM)] * 8,
-        out_specs=[spec(VMEM)] * 5,
-        compiler_params=params(),
-    )(hot_flags, owner_slot, expert_ids.T, route_slots.T, gate_probs.T, tokens, grad_out, hot_gate, hot_up, hot_down)
-
     packed = half + SIDE
     lines = 8 * NZ
     hot_rows = 2 * NX * HCAP
-    back_cold, back_hot, back_w, rows, d_gate, d_up, d_down = pl.pallas_call(
+    pos, back_cold, back_hot, back_w, rows, d_gate, d_up, d_down = pl.pallas_call(
         layer_kernel,
-        out_shape=(shape(GROUPS * NZ, 8, packed), shape(NX, HCAP, wide), shape(NZ, 16, width), shape(2 * CHIPS, 8, wide)) + (shape(16 * CHIPS, ff),) * 3,
-        in_specs=[spec(pl.ANY)] * 4 + [spec(VMEM)] * 3,
-        out_specs=[spec(pl.ANY)] * 7,
+        out_shape=(shape(2, token_count, dtype=jnp.int32), shape(GROUPS * NZ, 8, packed), shape(NX, HCAP, wide), shape(NZ, 16, width), shape(2 * CHIPS, 8, wide)) + (shape(16 * CHIPS, ff),) * 3,
+        in_specs=[spec(pltpu.SMEM)] * 2 + [spec(VMEM)] * 8 + [spec(pl.ANY)] * 3,
+        out_specs=[spec(VMEM)] + [spec(pl.ANY)] * 7,
         scratch_shapes=[
+            VMEM((ff, width), BF16), VMEM((ff, width), BF16), VMEM((ff, width), BF16),
+            VMEM((GROUPS * NZ, 8, wide), BF16), VMEM((HCAP, wide), BF16), VMEM((HCAP, width), BF16), VMEM((16, width), BF16),
             VMEM((2 * CHIPS, 8, wide), BF16), VMEM((hot_rows, wide), BF16), VMEM((hot_rows, width), BF16), VMEM((units, width), BF16),
             VMEM((16 * CHIPS, ff), BF16), VMEM((16 * CHIPS, ff), BF16), VMEM((16 * CHIPS, ff), BF16), VMEM((2 * hot_rows, units), BF16),
             VMEM((16 * CHIPS, packed), F32), VMEM((2 * GROUPS, lines, packed), BF16), VMEM((2 * GROUPS, lines, packed), BF16),
@@ -502,10 +520,10 @@
             VMEM((hot_rows, wide), F32), VMEM((NX * HCAP, wide), BF16), VMEM((NX * HCAP, wide), BF16), VMEM((NX * HCAP, wide), BF16), VMEM((NZ * 16, width), F32), VMEM((NZ * 16, width), BF16), VMEM((NZ * 16, width), BF16), VMEM((NZ * 16, width), BF16),
             dma((3,)), dma, dma((GROUPS,)), dma((2,)), dma((2,)), dma, dma, dma((GROUPS,)), dma((GROUPS,)),
             dma((2 * GROUPS + 2,)), dma((2 * GROUPS + 2,)), dma((2 * GROUPS + 1,)), dma((2 * GROUPS + 1,)),
-            dma((GROUPS,)), dma((GROUPS,)), dma, dma, dma, dma, dma, dma, dma((2,)), dma((2,)), dma((2,)), dma((4,)),
+            dma((GROUPS,)), dma((GROUPS,)), dma, dma, dma, dma, dma, dma, dma((2,)), dma((2,)), dma((2,)), dma((4,)), dma((3,)),
         ],
         compiler_params=params(collective_id=0, has_side_effects=True),
-    )(cold.reshape(CHIPS, 8, wide), hot_x, hot_g, weights, cold_gate[0], cold_up[0], cold_down[0])
+    )(hot_flags, owner_slot, expert_ids.T, route_slots.T, gate_probs.T, tokens, grad_out, hot_gate, hot_up, hot_down, cold_gate[0], cold_up[0], cold_down[0])
 
     mine = token_count // 2
     own_rows, other_rows, h_gate, h_up, h_down = pl.pallas_call(

time: 128 us -> 115 us (0.90)
  Pallas kernels: 124 us -> 109 us
  waiting for transfers between devices: 0.47 us -> 2.99 us
    pallas_call x2 -> x1, Pallas kernels: 113 us -> 98.1 us  [local(): pl.pallas_call(layer_kernel, out_shape=(shape(2, token_count, dtype=jnp.i...]
    ppermute x1, waiting for transfers between devices: 0.47 us -> 2.99 us  [local(): swapped = lax.ppermute(other_rows, 'pair', [(0, 1), (1, 0)])]
  transfers between devices with their start and end apart: 1 -> 1, of which waited for: 1 -> 1; matrix products, arithmetic and copies ran while one was open for 0% -> 0% of each run, Pallas kernels for 6% -> 7%
where the time goes in v4:
time: 115 us; the launch traced here: 114 us
  Pallas kernels  109 us (95%)
  waiting for transfers between devices  2.99 us (3%)
  local copies, waits for them, and re-layouts  1.41 us (1%)
    pallas_call x1, Pallas kernels, local(): pl.pallas_call(layer_kernel, out_shape=(shape(2, token_count, dtype=jnp.i...  98.1 us
    pallas_call x1, Pallas kernels, local(): pl.pallas_call(weight_kernel, out_shape=(shape(ff, width),) * 3, in_specs...  7.66 us
    pallas_call x1, Pallas kernels, local(): pl.pallas_call(unpack_kernel, out_shape=(shape(mine, wide, dtype=F32), sh...  3.57 us
    ppermute x1, waiting for transfers between devices, local(): swapped = lax.ppermute(other_rows, 'pair', [(0, 1), (1, 0)])  2.99 us
  transfers between devices with their start and end apart: 1, of which 1 were waited for; matrix products, arithmetic and copies ran while one was open for 0% of the time, Pallas kernels for 7%

profile of v4, /device:TPU:1, one launch (start us, length us, event | category | flops | bytes accessed | tf_op | source)
XLA Modules:
  0.0 114.5 jit_solution(12990518021165804377)
XLA Ops:
  0.6 98.1 %shard_map.188 = (s32[2,192]{1,0:T(2,128)}, bf16[32,8,1024]{2,1,0:T(8,128)(2,1)}, bf16[4,48,1920]{2,1,0:T(8,128)(2,1)}, bf16[8,16,1792]{2,1,0:T(8,128)(2,1)}, bf...) custom-call(s32[65]{0:T(128)} %flags.1, s32[65]{0:T(128)} %owner.1, ...), custom_call_target="tpu_custom_call" | custom-call | tf_op jit(solution)/shard_map/pallas_call | solution.py:508
  98.8 3.6 %shard_map.189 = (f32[96,1920]{1,0:T(8,128)}, bf16[96,1920]{1,0:T(8,128)(2,1)}, bf16[5,1792]{1,0:T(8,128)(2,1)}, bf16[5,1792]{1,0:T(8,128)(2,1)}, bf16[5,1792]{1,0:T(8,128)(2,1)}) custom-call(s32[2,192]{1,0:T(2,128)} %get-tuple-element.24.pos, bf16[256,1024]{1,0:T(8,128)(2,1)} %bitcast.16, bf16[192,1920]{1,0:T(8,128)(2,1)} %bitcast.15, ...), custom_call_target="tpu_custom_call" | custom-call | tf_op jit(solution)/shard_map/pallas_call | solution.py:529
  102.3 0.0 collective-permute-start
  102.3 0.0 copy-start
  102.3 7.7 %shard_map.190 = (bf16[320,1792]{1,0:T(8,128)(2,1)}, bf16[320,1792]{1,0:T(8,128)(2,1)}, bf16[320,1792]{1,0:T(8,128)(2,1)}) custom-call(bf16[1024,1920]{1,0:T(8,128)(2,1)} %bitcast.20, bf16[1024,320]{1,0:T(8,128)(2,1)} %get-tuple-element.31.d_gate, bf16[1024,320]{1,0:T(8,128)(2,1)} %get-tuple-element.32.d_up, bf16[1024,320]{1,0:T(8,128)(2,1)} %get-tuple-element.33.d_down), custom_call_target="tpu_custom_call" | custom-call | flops 3523215360 | bytes 9338880 | tf_op jit(solution)/shard_map/pallas_call | solution.py:540
  110.0 3.0 %collective-permute-done = bf16[96,1920]{1,0:T(8,128)(2,1)S(1)} collective-permute-done((bf16[96,1920]{1,0:T(8,128)(2,1)}, bf16[96,1920]{1,0:T(8,128)(2,1)S(1)}, u32[]{:S(2)}, u32[]{:S(2)}) %collective-permute-start) | collective-permute-done | bytes 368672 | tf_op jit(solution)/shard_map/ppermute | solution.py:538
  113.0 0.0 copy-done
  113.0 0.1 convert_add_fusion
  113.1 0.8 slice.12
  113.8 0.6 copy.21
  (1 shorter events, 0.0 us)
Async XLA Ops:
  102.3 10.7 %collective-permute-start = (bf16[96,1920]{1,0:T(8,128)(2,1)}, bf16[96,1920]{1,0:T(8,128)(2,1)S(1)}, u32[]{:S(2)}, u32[]{:S(2)}) collective-permute-start(bf16[96,1920]{1,0:T(8,128)(2,1)} %get-tuple-element.29), channel_id=1, source_target_pairs={{0,1},{1,0},{2,3},{3,2},{4,5},{5,4},{6,7},{7,6},{8,9},{9,8},{10,11... | collective-permute-start | bytes 1105928 | tf_op jit(solution)/shard_map/ppermute | solution.py:538
  102.3 10.7 %copy-start = (f32[96,1920]{1,0:T(8,128)S(1)}, f32[96,1920]{1,0:T(8,128)}, u32[]{:S(2)}) copy-start(f32[96,1920]{1,0:T(8,128)} %get-tuple-element.28) | copy-start | bytes 2211844

commit v5 on v4

--- a/solution.py
+++ b/solution.py
@@ -86,8 +86,8 @@
 
 def layer_kernel(
     flags, owner, ids, slots, probs_in, tokens, grad, gate, up, down, c_gate_in, c_up_in, c_down_in,
-    pos, back_cold, back_hot, back_w, cold_out, gate_out, up_out, down_out,
-    c_gate, c_up, c_down, cold_in, hot_x_in, hot_g_in, w_in, cold, hot_x, hot_g, w, d_gate, d_up, d_down, d_hot, ret, away, side, pass_on, passed, final,
+    own_rows, other_rows, back_w, cold_out, gate_out, up_out, down_out,
+    pos, back_cold, back_hot, total, c_gate, c_up, c_down, cold_in, hot_x_in, hot_g_in, w_in, cold, hot_x, hot_g, w, d_gate, d_up, d_down, d_hot, ret, away, side, pass_on, passed, final,
     hot_ret, hot_away, hot_side, hot_sum, w_ret, w_away, w_side, w_sum,
     own, cold_send, cold_recv, hot_send, hot_recv, w_send, w_recv, near_send, near_recv, over_send, over_recv,
     side_send, side_recv, pass_send, pass_recv, back_send, back_recv, hb_send, hb_recv, wb_send, wb_recv, wy_send, wy_recv, one_send, out_sem, load_sem,
@@ -135,21 +135,21 @@
     parts = [gate[...].astype(F32), up[...].astype(F32), down[...].astype(F32), rest]
     w_in[...] = jnp.concatenate(parts, axis=0).astype(BF16)
 
-    def pack(j):
-        base = (lax.rem(x + pair + 2 * (j // NY), NX) * NY + lax.rem(y + j % NY, NY)) * NZ
-        row = iota((8 * NZ, token_count), 0)
+    def pack():
+        row = iota((8 * NZ * GROUPS, token_count), 0)
         within = row & 7
-        want = (base + (row >> 3)) * CAP + (within & 3)
+        group = lax.div(row, 8 * NZ)
+        to_x = lax.rem(x + pair + 2 * lax.div(group, NY), NX)
+        to_y = lax.rem(y + lax.rem(group, NY), NY)
+        want = ((to_x * NY + to_y) * NZ + lax.rem(lax.div(row, 8), NZ)) * CAP + (within & 3)
         first, second = pos[0:1, :] == want, pos[1:2, :] == want
         match = first | second
         rows = jnp.dot(one_hot(match & (within < CAP)), tokens[...], preferred_element_type=F32)
         rows += jnp.dot(one_hot(match & (within >= CAP)), grad[...], preferred_element_type=F32)
-        at = slice(j * NZ, (j + 1) * NZ)
-        cold_in[at, :, :width] = rows.astype(BF16).reshape(NZ, 8, width)
-        cold_in[at, :, width:] = scale_of(first, second).reshape(NZ, 8, SIDE)
-
-    for j in range(GROUPS):
-        pack(j)
+        cold_in[:, :, :width] = rows.astype(BF16).reshape(GROUPS * NZ, 8, width)
+        cold_in[:, :, width:] = scale_of(first, second).reshape(GROUPS * NZ, 8, SIDE)
+
+    pack()
     pl.semaphore_wait(barrier, CHIPS + 1)
 
     def hot_at(which, k):
@@ -389,14 +389,11 @@
         copy.wait()
     relay(0)
     relay(1)
-    for j in range(2, GROUPS):
-        if j == 2:
-            receive(2)
-        if j == 3:
-            compute(0)
-            receive(3)
-    if GROUPS == 2:
-        compute(0)
+    if GROUPS > 2:
+        receive(2)
+    compute(0)
+    if GROUPS > 2:
+        receive(3)
     compute(GROUPS // 2)
     return_weights()
     return_hot()
@@ -441,55 +438,50 @@
         remote(cold_in.at[0], cold_in.at[0], one_send.at[0], back_recv, sibling).wait_send()
         remote(final.at[0], final.at[0], one_send.at[1], back_recv, sibling).wait_send()
 
-
-def unpack_kernel(pos, cold, hot, w, own_rows, other_rows, g_gate, g_up, g_down, total):
-    token_count = pos.shape[1]
-    half = cold.shape[1] - SIDE
-    width = 2 * half
-    rows = cold.shape[0]
-    mine = token_count // 2
-    pair, _, x, y, _ = place()
+    rows = 8 * NZ * GROUPS
+    returned = back_cold[...].reshape(rows, half + SIDE)
+    hot_back = back_hot[...].reshape(NX * HCAP, width + SIDE)
     row = iota((rows, token_count), 0)
     within = row & 7
     group = lax.div(row, 8 * NZ)
-    owner_x = lax.rem(x + pair + 2 * lax.div(group, NY), NX)
-    owner_y = lax.rem(y + lax.rem(group, NY), NY)
-    owner = (owner_x * NY + owner_y) * NZ + lax.rem(lax.div(row, 8), NZ)
-    want = owner * CAP + (within & 3)
+    from_x = lax.rem(x + pair + 2 * lax.div(group, NY), NX)
+    from_y = lax.rem(y + lax.rem(group, NY), NY)
+    chip = (from_x * NY + from_y) * NZ + lax.rem(lax.div(row, 8), NZ)
+    want = chip * CAP + (within & 3)
     first = pos[0:1, :] == want
     second = pos[1:2, :] == want
     match = first | second
     pick_low = one_hot(match & (within < CAP))
     pick_high = one_hot(match & (within >= CAP))
-    hot_rows = hot.shape[0]
-    hot_want = CHIPS * CAP + lax.rem(iota((hot_rows, token_count), 0), HCAP)
+    hot_want = CHIPS * CAP + lax.rem(iota((NX * HCAP, token_count), 0), HCAP)
     hot_first = pos[0:1, :] == hot_want
     hot_second = pos[1:2, :] == hot_want
     pick_hot = one_hot(hot_first | hot_second)
     for low, cold_pick in ((0, pick_low), (half, pick_high)):
-        part = lax.dot_general(cold_pick, cold[:, :half], ROWS, preferred_element_type=F32)
-        part += lax.dot_general(pick_hot, hot[:, low : low + half], ROWS, preferred_element_type=F32)
+        part = lax.dot_general(cold_pick, returned[:, :half], ROWS, preferred_element_type=F32)
+        part += lax.dot_general(pick_hot, hot_back[:, low : low + half], ROWS, preferred_element_type=F32)
         total[:, low : low + half] = part
     is_x = within < CAP
     values = []
     for a, b in ((first, hot_first), (second, hot_second)):
-        value = lax.dot_general(one_hot(a & is_x), cold[:, half:], ROWS, preferred_element_type=F32)
-        values.append(value + lax.dot_general(one_hot(b), hot[:, width:], ROWS, preferred_element_type=F32))
+        value = lax.dot_general(one_hot(a & is_x), returned[:, half:], ROWS, preferred_element_type=F32)
+        values.append(value + lax.dot_general(one_hot(b), hot_back[:, width:], ROWS, preferred_element_type=F32))
     total[:, width:] = jnp.where(iota((token_count, SIDE), 1) == 0, values[0], values[1])
-    own_rows[...] = total[pl.ds(pl.multiple_of(pair * mine, 8), mine), :]
-    other_rows[...] = total[pl.ds(pl.multiple_of((1 - pair) * mine, 8), mine), :].astype(BF16)
-    grads = w[0].astype(F32)
-    for k in range(1, w.shape[0]):
-        grads += w[k].astype(F32)
-    g_gate[...] = grads[0:UNIT].astype(BF16)
-    g_up[...] = grads[UNIT : 2 * UNIT].astype(BF16)
-    g_down[...] = grads[2 * UNIT : 3 * UNIT].astype(BF16)
-
-
-def weight_kernel(cold, d_gate, d_up, d_down, g_gate, g_up, g_down):
+    count = token_count // 2
+    own_rows[...] = total[pl.ds(pl.multiple_of(pair * count, 16), count), :]
+    other_rows[...] = total[pl.ds(pl.multiple_of((1 - pair) * count, 16), count), :].astype(BF16)
+
+
+def weight_kernel(cold, d_gate, d_up, d_down, w, g_gate, g_up, g_down, h_gate, h_up, h_down):
     width = g_gate.shape[1]
     for grads, out in ((d_gate, g_gate), (d_up, g_up), (d_down, g_down)):
         out[...] = lax.dot_general(grads[...], cold[:, :width], ROWS, preferred_element_type=F32).astype(BF16)
+    sums = w[0].astype(F32)
+    for k in range(1, w.shape[0]):
+        sums += w[k].astype(F32)
+    h_gate[...] = sums[0:UNIT].astype(BF16)
+    h_up[...] = sums[UNIT : 2 * UNIT].astype(BF16)
+    h_down[...] = sums[2 * UNIT : 3 * UNIT].astype(BF16)
 
 
 def shape(*dims, dtype=BF16):
@@ -505,12 +497,13 @@
     packed = half + SIDE
     lines = 8 * NZ
     hot_rows = 2 * NX * HCAP
-    pos, back_cold, back_hot, back_w, rows, d_gate, d_up, d_down = pl.pallas_call(
+    own_rows, other_rows, back_w, rows, d_gate, d_up, d_down = pl.pallas_call(
         layer_kernel,
-        out_shape=(shape(2, token_count, dtype=jnp.int32), shape(GROUPS * NZ, 8, packed), shape(NX, HCAP, wide), shape(NZ, 16, width), shape(2 * CHIPS, 8, wide)) + (shape(16 * CHIPS, ff),) * 3,
+        out_shape=(shape(token_count // 2, wide, dtype=F32), shape(token_count // 2, wide), shape(NZ, 16, width), shape(2 * CHIPS, 8, wide)) + (shape(16 * CHIPS, ff),) * 3,
         in_specs=[spec(pltpu.SMEM)] * 2 + [spec(VMEM)] * 8 + [spec(pl.ANY)] * 3,
-        out_specs=[spec(VMEM)] + [spec(pl.ANY)] * 7,
+        out_specs=[spec(VMEM)] * 2 + [spec(pl.ANY)] * 5,
         scratch_shapes=[
+            VMEM((2, token_count), jnp.int32), VMEM((GROUPS * NZ, 8, packed), BF16), VMEM((NX, HCAP, wide), BF16), VMEM((token_count, wide), F32),
             VMEM((ff, width), BF16), VMEM((ff, width), BF16), VMEM((ff, width), BF16),
             VMEM((GROUPS * NZ, 8, wide), BF16), VMEM((HCAP, wide), BF16), VMEM((HCAP, width), BF16), VMEM((16, width), BF16),
             VMEM((2 * CHIPS, 8, wide), BF16), VMEM((hot_rows, wide), BF16), VMEM((hot_rows, width), BF16), VMEM((units, width), BF16),
@@ -525,26 +518,16 @@
         compiler_params=params(collective_id=0, has_side_effects=True),
     )(hot_flags, owner_slot, expert_ids.T, route_slots.T, gate_probs.T, tokens, grad_out, hot_gate, hot_up, hot_down, cold_gate[0], cold_up[0], cold_down[0])
 
-    mine = token_count // 2
-    own_rows, other_rows, h_gate, h_up, h_down = pl.pallas_call(
-        unpack_kernel,
-        out_shape=(shape(mine, wide, dtype=F32), shape(mine, wide)) + (shape(UNIT, width),) * 3,
-        in_specs=[spec(VMEM)] * 4,
-        out_specs=[spec(VMEM)] * 5,
-        scratch_shapes=[VMEM((token_count, wide), F32)],
-        compiler_params=params(),
-    )(pos, back_cold.reshape(GROUPS * NZ * 8, packed), back_hot.reshape(NX * HCAP, wide), back_w)
-
     swapped = lax.ppermute(other_rows, "pair", [(0, 1), (1, 0)])
     count = 16 * CHIPS
-    g_gate, g_up, g_down = pl.pallas_call(
+    g_gate, g_up, g_down, h_gate, h_up, h_down = pl.pallas_call(
         weight_kernel,
-        out_shape=(shape(ff, width),) * 3,
-        in_specs=[spec(VMEM)] * 4,
-        out_specs=[spec(VMEM)] * 3,
+        out_shape=(shape(ff, width),) * 3 + (shape(UNIT, width),) * 3,
+        in_specs=[spec(VMEM)] * 5,
+        out_specs=[spec(VMEM)] * 6,
         cost_estimate=pl.CostEstimate(flops=6 * count * ff * width, bytes_accessed=2 * count * (wide + 3 * ff) + 6 * ff * width, transcendentals=0),
         compiler_params=params(),
-    )(rows.reshape(count, wide), d_gate, d_up, d_down)
+    )(rows.reshape(count, wide), d_gate, d_up, d_down, back_w)
     summed = own_rows + swapped.astype(F32)
     return (summed[:, :width].astype(BF16), summed[:, width : width + 2], g_gate[None], g_up[None], g_down[None], h_gate, h_up, h_down)
 

time: 115 us -> 112 us (0.974)
    pallas_call x3 -> x2, Pallas kernels: 109 us -> 108 us  [the longest x1 100 us: local(): pl.pallas_call(layer_kernel, out_shape=(shape(token_count // 2, wide, dty...]
where the time goes in v5:
time: 112 us
  Pallas kernels  108 us (96%)
  waiting for transfers between devices  2.2 us (2%)
  local copies, waits for them, and re-layouts  1.41 us (1%)
    pallas_call x1, Pallas kernels, local(): pl.pallas_call(layer_kernel, out_shape=(shape(token_count // 2, wide, dty...  100 us
    pallas_call x1, Pallas kernels, local(): pl.pallas_call(weight_kernel, out_shape=(shape(ff, width),) * 3 + (shape(...  7.77 us
  transfers between devices with their start and end apart: 1, of which 1 were waited for; matrix products, arithmetic and copies ran while one was open for 0% of the time, Pallas kernels for 7%

profile of v5, /device:TPU:1, one launch (start us, length us, event | category | flops | bytes accessed | tf_op | source)
XLA Modules:
  0.0 112.3 jit_solution(13202258715875777239)
XLA Ops:
  0.6 100.1 %shard_map.188 = (f32[96,1920]{1,0:T(8,128)}, bf16[96,1920]{1,0:T(8,128)(2,1)}, bf16[8,16,1792]{2,1,0:T(8,128)(2,1)}, bf16[128,8,1920]{2,1,0:T(8,128)(2,1)}, bf1...) custom-call(s32[65]{0:T(128)} %flags.1, s32[65]{0:T(128)} %owner.1, ...), custom_call_target="tpu_custom_call" | custom-call | tf_op jit(solution)/shard_map/pallas_call | solution.py:500
  100.7 0.1 collective-permute-start
  100.8 0.0 copy-start
  100.8 7.8 %shard_map.189 = (bf16[320,1792]{1,0:T(8,128)(2,1)}, bf16[320,1792]{1,0:T(8,128)(2,1)}, bf16[320,1792]{1,0:T(8,128)(2,1)}, bf16[5,1792]{1,0:T(8,128)(2,1)}, bf16...) custom-call(bf16[1024,1920]{1,0:T(8,128)(2,1)} %bitcast.16, bf16[1024,320]{1,0:T(8,128)(2,1)} %get-tuple-element.24.d_gate, ...), custom_call_target="tpu_custom_call" | custom-call | flops 3523215360 | bytes 9338880 | tf_op jit(solution)/shard_map/pallas_call | solution.py:523
  108.6 2.2 %collective-permute-done = bf16[96,1920]{1,0:T(8,128)(2,1)S(1)} collective-permute-done((bf16[96,1920]{1,0:T(8,128)(2,1)}, bf16[96,1920]{1,0:T(8,128)(2,1)S(1)}, u32[]{:S(2)}, u32[]{:S(2)}) %collective-permute-start) | collective-permute-done | bytes 368672 | tf_op jit(solution)/shard_map/ppermute | solution.py:521
  110.8 0.0 copy-done
  110.8 0.1 convert_add_fusion
  110.9 0.8 slice.12
  111.6 0.6 copy.21
  (1 shorter events, 0.0 us)
Async XLA Ops:
  100.7 10.1 %collective-permute-start = (bf16[96,1920]{1,0:T(8,128)(2,1)}, bf16[96,1920]{1,0:T(8,128)(2,1)S(1)}, u32[]{:S(2)}, u32[]{:S(2)}) collective-permute-start(bf16[96,1920]{1,0:T(8,128)(2,1)} %get-tuple-element.22), channel_id=1, source_target_pairs={{0,1},{1,0},{2,3},{3,2},{4,5},{5,4},{6,7},{7,6},{8,9},{9,8},{10,11... | collective-permute-start | bytes 1105928 | tf_op jit(solution)/shard_map/ppermute | solution.py:521
  100.8 10.0 %copy-start = (f32[96,1920]{1,0:T(8,128)S(1)}, f32[96,1920]{1,0:T(8,128)}, u32[]{:S(2)}) copy-start(f32[96,1920]{1,0:T(8,128)} %get-tuple-element.21) | copy-start | bytes 2211844

commit v6 on v5

--- a/solution.py
+++ b/solution.py
@@ -395,14 +395,17 @@
     if GROUPS > 2:
         receive(3)
     compute(GROUPS // 2)
-    return_weights()
-    return_hot()
+    if GROUPS == 2:
+        return_weights()
+        return_hot()
     pass_over(0)
     pass_over(1)
     if GROUPS > 2:
         relay(2)
+        return_weights()
         compute(1)
         relay(3)
+        return_hot()
         give_back(0)
         give_back(1)
         compute(3)

time: 112 us -> 109 us (0.973)
  Pallas kernels: 108 us -> 105 us
    pallas_call x1, Pallas kernels: 100 us -> 97.2 us  [local(): pl.pallas_call(layer_kernel, out_shape=(shape(token_count // 2, wide, dty...]
where the time goes in v6:
time: 109 us
  Pallas kernels  105 us (96%)
  waiting for transfers between devices  1.99 us (2%)
  local copies, waits for them, and re-layouts  1.41 us (1%)
    pallas_call x1, Pallas kernels, local(): pl.pallas_call(layer_kernel, out_shape=(shape(token_count // 2, wide, dty...  97.2 us
    pallas_call x1, Pallas kernels, local(): pl.pallas_call(weight_kernel, out_shape=(shape(ff, width),) * 3 + (shape(...  7.77 us
  transfers between devices with their start and end apart: 1, of which 1 were waited for; matrix products, arithmetic and copies ran while one was open for 0% of the time, Pallas kernels for 7%

profile of v6, /device:TPU:1, one launch (start us, length us, event | category | flops | bytes accessed | tf_op | source)
XLA Modules:
  0.0 109.2 jit_solution(11780719876601427343)
XLA Ops:
  0.6 97.2 %shard_map.188 = (f32[96,1920]{1,0:T(8,128)}, bf16[96,1920]{1,0:T(8,128)(2,1)}, bf16[8,16,1792]{2,1,0:T(8,128)(2,1)}, bf16[128,8,1920]{2,1,0:T(8,128)(2,1)}, bf1...) custom-call(s32[65]{0:T(128)} %flags.1, s32[65]{0:T(128)} %owner.1, ...), custom_call_target="tpu_custom_call" | custom-call | tf_op jit(solution)/shard_map/pallas_call | solution.py:503
  97.9 0.1 collective-permute-start
  98.0 0.0 copy-start
  98.0 7.8 %shard_map.189 = (bf16[320,1792]{1,0:T(8,128)(2,1)}, bf16[320,1792]{1,0:T(8,128)(2,1)}, bf16[320,1792]{1,0:T(8,128)(2,1)}, bf16[5,1792]{1,0:T(8,128)(2,1)}, bf16...) custom-call(bf16[1024,1920]{1,0:T(8,128)(2,1)} %bitcast.16, bf16[1024,320]{1,0:T(8,128)(2,1)} %get-tuple-element.24.d_gate, ...), custom_call_target="tpu_custom_call" | custom-call | flops 3523215360 | bytes 9338880 | tf_op jit(solution)/shard_map/pallas_call | solution.py:526
  105.8 2.0 %collective-permute-done = bf16[96,1920]{1,0:T(8,128)(2,1)S(1)} collective-permute-done((bf16[96,1920]{1,0:T(8,128)(2,1)}, bf16[96,1920]{1,0:T(8,128)(2,1)S(1)}, u32[]{:S(2)}, u32[]{:S(2)}) %collective-permute-start) | collective-permute-done | bytes 368672 | tf_op jit(solution)/shard_map/ppermute | solution.py:524
  107.8 0.0 copy-done
  107.8 0.1 convert_add_fusion
  107.8 0.8 slice.12
  108.6 0.6 copy.21
  (1 shorter events, 0.0 us)
Async XLA Ops:
  97.9 9.9 %collective-permute-start = (bf16[96,1920]{1,0:T(8,128)(2,1)}, bf16[96,1920]{1,0:T(8,128)(2,1)S(1)}, u32[]{:S(2)}, u32[]{:S(2)}) collective-permute-start(bf16[96,1920]{1,0:T(8,128)(2,1)} %get-tuple-element.22), channel_id=1, source_target_pairs={{0,1},{1,0},{2,3},{3,2},{4,5},{5,4},{6,7},{7,6},{8,9},{9,8},{10,11... | collective-permute-start | bytes 1105928 | tf_op jit(solution)/shard_map/ppermute | solution.py:524
  98.0 9.8 %copy-start = (f32[96,1920]{1,0:T(8,128)S(1)}, f32[96,1920]{1,0:T(8,128)}, u32[]{:S(2)}) copy-start(f32[96,1920]{1,0:T(8,128)} %get-tuple-element.21) | copy-start | bytes 2211844
